TPU v7x, 128 devices: a whole 4x4x4 slice. The times are simulated.
128 devices in a mesh: frames: 4 (over y_lo, core), hidden: 32 (over y_hi, x, z).
Axes of the slice: x: 4, y: 4 (y_hi: 2, y_lo: 2; y = y_hi * 2 + y_lo), z: 4, core: 2. Of those that a mesh axis runs over, the one named last changes fastest.
Arguments:
- frames_in: bfloat16 [2048, 2048], P('frames', 'hidden'), may hold values from -6 to 6
- in_gain: float32 [2048], replicated, may hold values from 0.1 to 1.9
- w_in: bfloat16 [2048, 8192], P(None, 'hidden'), may hold values from -0.125 to 0.125
- w_out: bfloat16 [8192, 2048], P('hidden'), may hold values from -0.0625 to 0.0625
- out_gain: float32 [2048], replicated, may hold values from 0.1 to 1.9
- table: bfloat16 [151936, 2048], P(('frames', 'hidden')), may hold values from -8 to 8
Outputs:
- soft_embed: bfloat16 [2048, 2048], P('frames', 'hidden')
- log_total: float32 [2048], P('frames')
All inputs are finite; a program needn't handle non-finite values.
Results may differ from a plain program's by a relative error of at most 0.0085.
The roundings to bfloat16 on the way count: a program that leaves them out, or rounds other values in their place, can miss the bound.
Values may be sent and summed in bfloat16 or wider, within the bound.
A program may use at most 128 MiB of HBM per device.

v0:
```python
import math

import jax
import jax.numpy as jnp
from jax import lax
from jax.sharding import PartitionSpec as P


def rms_scale(values, gain_vec):
    mean_sq = jnp.mean(values * values, axis=-1, keepdims=True)
    return values * lax.rsqrt(mean_sq + 1e-06) * gain_vec


def shards(frames_in, in_gain, w_in, w_out, out_gain, table):
    full_rows = lax.all_gather(frames_in, "hidden", axis=1, tiled=True)
    inputs = full_rows.astype(jnp.float32)
    normed = rms_scale(inputs, in_gain).astype(jnp.bfloat16)
    hidden = jax.nn.gelu(
        jnp.dot(normed, w_in, preferred_element_type=jnp.float32), approximate=True
    ).astype(jnp.bfloat16)
    ffn_partial = jnp.dot(hidden, w_out, preferred_element_type=jnp.float32)
    encoded = lax.psum(ffn_partial, "hidden") + inputs
    latent = rms_scale(encoded, out_gain).astype(jnp.bfloat16)
    score_scale = 5.0 / math.sqrt(latent.shape[1])
    contract_rows = (((0,), (0,)), ((), ()))
    contract_feat = (((1,), (1,)), ((), ()))
    vocab_rows = lax.all_gather(table, "frames", axis=0, tiled=True)
    scores = (
        lax.dot_general(vocab_rows, latent, contract_feat, preferred_element_type=jnp.float32)
        * score_scale
    )
    local_top = jnp.max(scores, axis=0)
    highest = lax.pmax(local_top, "hidden")
    exponent = jnp.exp(scores - highest[None, :])
    row_total = lax.psum(jnp.sum(exponent, axis=0), "hidden")
    weights = exponent.astype(jnp.bfloat16)
    feature_share = lax.psum_scatter(
        lax.dot_general(vocab_rows, weights, contract_rows, preferred_element_type=jnp.float32),
        "hidden",
        scatter_dimension=0,
        tiled=True,
    )
    soft_embed = (feature_share.T / row_total[:, None]).astype(jnp.bfloat16)
    log_total = highest + jnp.log(row_total)
    return (soft_embed, log_total)


def solution(mesh):
    placed = (
        P("frames", "hidden"),
        P(),
        P(None, "hidden"),
        P("hidden", None),
        P(),
        P(("frames", "hidden"), None),
    )
    return jax.shard_map(
        shards,
        mesh=mesh,
        in_specs=placed,
        out_specs=(P("frames", "hidden"), P("frames")),
        check_vma=False,
    )
```

profile of v0, /device:TPU:0, one launch (start us, length us, event | category | flops | bytes accessed | tf_op | source)
XLA Modules:
  0.0 813.1 jit_solution(8360284355940004372)
XLA Ops:
  8.0 0.0 copy-start
  8.0 0.0 copy-start.2
  8.0 0.0 all-gather.4.cloned.1.call-start
  8.1 0.7 all-gather.4.cloned.1.call-update
  8.8 0.0 all-reduce.2.cloned.1.call-start
  8.8 76.6 %all-gather.4.cloned.1.call-done = bf16[512,2048]{0,1:T(8,128)(2,1)} async-done(((bf16[512,64]{0,1:T(8,128)(2,1)}), bf16[512,2048]{0,1:T(8,128)(2,1)}) %all-gather.4.cloned.1.call-update) | async-done | bytes 2097168 | tf_op jit(solution)/shard_map/all_gather | solution.py:15
  85.4 2.9 copy.12
  88.3 0.5 fusion.5
  88.8 0.0 copy-done
  88.8 5.6 fusion.30
  94.5 0.0 all-reduce.2.cloned.1.call-update
  94.5 0.0 all-gather.6.cloned.1.call-start
  94.5 0.5 all-gather.6.cloned.1.call-update
  95.1 0.2 reduce-scatter.4.cloned.1.call-start
  95.3 362.9 %all-reduce.2.cloned.1.call-done = f32[512,2048]{1,0:T(8,128)} async-done(((f32[512,2048]{1,0:T(8,128)}), f32[512,2048]{1,0:T(8,128)}) %all-reduce.2.cloned.1.call-update) | async-done | bytes 4194320 | tf_op jit(solution)/shard_map/psum | solution.py:22
  458.2 2.8 multiply_reduce_fusion
  461.0 0.0 copy-start.3
  461.0 0.0 all-gather.6.cloned.1.call-done
  461.1 18.2 %reshape.25 = bf16[4748,2048]{1,0:T(8,128)(2,1)} reshape(bf16[4,1187,2048]{2,1,0:T(8,128)(2,1)} %all-gather.6.cloned.1.call-done) | data formatting | bytes 38895616
  479.3 17.2 %fusion.41 = (f32[512]{0:T(512)S(1)}, f32[512,4748]{0,1:T(8,128)}) fusion(bf16[4748,2048]{1,0:T(8,128)(2,1)} %reshape.25, f32[512,2048]{1,0:T(8,128)} %all-reduce.2.cloned.1.call-done, bf16[512,2048]{1,0:T(8,128)(2,1)S(1)} %copy.12, f32[2048]{0:T(1024)S(1)} %copy-done.3, f32[512]{0:T(512)S(1)} %add_rsqrt_fusion), kind=kOutput, calls=%fused_computation.43 | convolution fusion | flops 9967382528 | bytes 35475456 | tf_op jit(solution)/shard_map/dot_general | solution.py:29
  496.6 96.0 %pmax.7 = f32[512]{0:T(512)S(1)} all-reduce(f32[512]{0:T(512)S(1)} %get-tuple-element.8), channel_id=1, replica_groups=mesh['frames'=4,'hidden'=32] {'hidden'}, use_global_device_ids=true, to_apply=%region_4.0 | all-reduce | flops 512 | bytes 4096 | tf_op jit(solution)/shard_map/pmax | solution.py:33
  592.6 18.6 %fusion.8 = f32[2048,512]{0,1:T(8,128)} fusion(bf16[4748,2048]{1,0:T(8,128)(2,1)} %reshape.25, f32[512,4748]{0,1:T(8,128)} %get-tuple-element.9, f32[512]{0:T(512)S(1)} %pmax.7), kind=kOutput, calls=%fused_computation.14 | convolution fusion | flops 9962139648 | bytes 33368064 | tf_op jit(solution)/shard_map/dot_general | solution.py:38
  611.2 5.4 copy.14
  616.6 0.0 reduce-scatter.4.cloned.1.call-update
  616.6 0.0 copy-start.1
  616.7 5.2 fusion
  621.9 88.9 %psum.15 = f32[512]{0:T(512)S(1)} all-reduce(f32[512]{0:T(512)S(1)} %fusion), channel_id=1, replica_groups=mesh['frames'=4,'hidden'=32] {'hidden'}, use_global_device_ids=true, to_apply=%region_7.0 | all-reduce | flops 512 | bytes 4096 | tf_op jit(solution)/shard_map/psum | solution.py:35
  710.8 0.6 log_add_fusion
  711.4 92.7 %reduce-scatter.4.cloned.1.call-done = f32[64,512]{1,0:T(8,128)} async-done(((f32[2048,512]{1,0:T(8,128)}), f32[64,512]{1,0:T(8,128)}) %reduce-scatter.4.cloned.1.call-update) | async-done | bytes 131088
  804.1 1.0 copy.15
  805.1 0.1 fusion.36
  805.3 0.7 copy.13
  (5 shorter events, 0.0 us)
Async XLA Ops:
  8.0 80.8 %copy-start = (bf16[256,2048]{1,0:T(8,128)(2,1)S(1)}, bf16[256,2048]{1,0:T(8,128)(2,1)}, u32[]{:S(2)}) copy-start(bf16[256,2048]{1,0:T(8,128)(2,1)} %param.9) | copy-start | bytes 3145732
  8.0 80.8 %copy-start.2 = (f32[2048]{0:T(1024)S(1)}, f32[2048]{0:T(1024)}, u32[]{:S(2)}) copy-start(f32[2048]{0:T(1024)} %param.7) | copy-start | bytes 24580
  8.0 77.4 %all-gather.4.cloned.1.call-start = ((), (), s32[]{:S(2)}) async-start(), calls=%async_computation.1 | async-start | bytes 2162688 | tf_op jit(solution)/shard_map/all_gather | solution.py:15
  8.8 449.5 %all-reduce.2.cloned.1.call-start = ((), (), s32[]{:S(2)}) async-start(), calls=%async_computation.2 | async-start | bytes 8388608 | tf_op jit(solution)/shard_map/psum | solution.py:22
  94.5 366.6 %all-gather.6.cloned.1.call-start = ((), (), s32[]{:S(2)}) async-start(), calls=%async_computation.3 | async-start | bytes 24412160 | tf_op jit(solution)/shard_map/all_gather | solution.py:27
  95.1 709.0 %reduce-scatter.4.cloned.1.call-start = ((), (), s32[]{:S(2)}) async-start(), calls=%async_computation.4 | async-start | bytes 4325376
  461.0 18.3 %copy-start.3 = (f32[2048]{0:T(1024)S(1)}, f32[2048]{0:T(1024)}, u32[]{:S(2)}) copy-start(f32[2048]{0:T(1024)} %param.10) | copy-start | bytes 24580
  616.6 189.4 %copy-start.1 = (bf16[256,2048]{1,0:T(8,128)(2,1)S(1)}, bf16[256,2048]{1,0:T(8,128)(2,1)}, u32[]{:S(2)}) copy-start(bf16[256,2048]{1,0:T(8,128)(2,1)} %param.9) | copy-start | bytes 3145732
Sparse Core Ops, SparseCore 0:
  12.0 73.3 all-gather.3
  94.6 363.5 all-reduce.1
  616.8 187.2 reduce-scatter.3
Sparse Core Ops, SparseCore 1:
  96.6 172.4 all-gather.5
where the time goes:
time: 814 us; the launch traced here: 813 us
  waiting for transfers between devices  533 us (65%)
  blocking collectives  185 us (23%)
  matrix products  41.5 us (5%)
  local copies, waits for them, and re-layouts  28.3 us (3%)
  between operations  15.3 us (2%)
  other arithmetic  9.28 us (1%)
    psum x1, waiting for transfers between devices, shards(): encoded = lax.psum(ffn_partial, 'hidden') + inputs  363 us
    pmax x1, blocking collectives, shards(): highest = lax.pmax(local_top, 'hidden')  96 us
    unnamed x5, waiting for transfers between devices  93.9 us
    psum x1, blocking collectives, shards(): row_total = lax.psum(jnp.sum(exponent, axis=0), 'hidden')  88.9 us
    all_gather x1, waiting for transfers between devices, shards(): full_rows = lax.all_gather(frames_in, 'hidden', axis=1, tiled=True)  76.6 us
    unnamed x12, local copies, waits for them, and re-layouts  25.4 us
    dot_general x1, matrix products, shards(): lax.dot_general(vocab_rows, weights, contract_rows, preferred_element_typ...  18.6 us
    dot_general x1, matrix products, shards(): lax.dot_general(vocab_rows, latent, contract_feat, preferred_element_type...  17.2 us
  transfers between devices with their start and end apart: 4, of which 3 were waited for; matrix products, arithmetic and copies ran while one was open for 1% of the time, Pallas kernels for 0%

commit v1 on v0

v1 whole, which is shorter than its diff:
```python
import functools
import math

import jax
import jax.numpy as jnp
from jax import lax
from jax.experimental import pallas as pl
from jax.experimental.pallas import tpu as pltpu
from jax.sharding import PartitionSpec as P

MESH = pl.DeviceIdType.MESH
D = 2048
ROWS = 1187
HALF = 1216
VP = 2 * HALF
VT = 608
F32 = jnp.float32
BF16 = jnp.bfloat16
ALL = slice(None)


def coords():
    f = lax.axis_index("frames")
    h = lax.axis_index("hidden")
    return {
        "x": lax.rem(lax.div(h, 4), 4),
        "y": lax.div(h, 16) * 2 + lax.div(f, 2),
        "z": lax.rem(h, 4),
        "c": lax.rem(f, 2),
    }


def device(at):
    return (
        lax.rem(at["y"], 2) * 2 + at["c"],
        lax.div(at["y"], 2) * 16 + at["x"] * 4 + at["z"],
    )


def moved(me, dim, by):
    return device({**me, dim: lax.rem(me[dim] + by + 4, 4)})


class Links:
    def __init__(self, send_sems, recv_sems):
        self.send_sems, self.recv_sems, self.copies = send_sems, recv_sems, []

    def send(self, src, dst, to):
        k = len(self.copies)
        copy = pltpu.make_async_remote_copy(
            src_ref=src,
            dst_ref=dst,
            send_sem=self.send_sems.at[k],
            recv_sem=self.recv_sems.at[k],
            device_id=to,
            device_id_type=MESH,
        )
        copy.start()
        self.copies.append(copy)
        return copy

    def drain(self):
        for copy in self.copies:
            copy.wait_send()


def run(*streams):
    streams = list(streams)
    while streams:
        for stream in list(streams):
            try:
                next(stream)
            except StopIteration:
                streams.remove(stream)


def ring_gather(links, me, dim, view, low, high):
    i = me[dim]
    right, left = moved(me, dim, 1), moved(me, dim, -1)
    before, after = lax.rem(i + 3, 4), lax.rem(i + 1, 4)
    r_low = links.send(view(i, low), view(i, low), right)
    l_high = links.send(view(i, high), view(i, high), left)
    r_high = links.send(view(i, high), view(i, high), right)
    l_low = links.send(view(i, low), view(i, low), left)
    yield
    r_low.wait_recv()
    r_far = links.send(view(before, low), view(before, low), right)
    l_high.wait_recv()
    l_far = links.send(view(after, high), view(after, high), left)
    yield
    r_high.wait_recv()
    l_low.wait_recv()
    r_far.wait_recv()
    l_far.wait_recv()


def ring_reduce(links, me, dim, view, near, far, low, high, add):
    i = me[dim]
    right, left = moved(me, dim, 1), moved(me, dim, -1)
    before, after, across = lax.rem(i + 3, 4), lax.rem(i + 1, 4), lax.rem(i + 2, 4)
    r_far = links.send(view(across, low), far[0](low), right)
    l_far = links.send(view(across, high), far[1](high), left)
    r_high = links.send(view(after, high), near[0](high), right)
    l_low = links.send(view(before, low), near[1](low), left)
    yield
    r_far.wait_recv()
    add(after, low, [far[0]])
    r_low = links.send(view(after, low), near[0](low), right)
    l_far.wait_recv()
    add(before, high, [far[1]])
    l_high = links.send(view(before, high), near[1](high), left)
    yield
    r_high.wait_recv()
    l_high.wait_recv()
    add(i, high, [near[0], near[1]])
    l_low.wait_recv()
    r_low.wait_recv()
    add(i, low, [near[0], near[1]])


def greet(peers):
    barrier = pltpu.get_barrier_semaphore()
    for peer in peers:
        pl.semaphore_signal(barrier, inc=1, device_id=peer, device_id_type=MESH)
    pl.semaphore_wait(barrier, len(peers))


def ffn_lead(sel):
    return tuple(ALL if sel[d] is None else sel[d] for d in ("w", "x", "z"))


def ffn_kernel(
    x_ref, gin_ref, win_ref, wout_ref, gout_ref, lat_ref,
    xb, xs, part, far_a, near_a, far_b, near_b, far_c, near_c, far_d, near_d, wrecv, ssem, rsem,
):
    me = coords()
    me_w = lax.div(me["y"], 2)
    opposite = moved(me, "y", 2)
    greet(
        [moved(me, "x", 1), moved(me, "x", -1), moved(me, "z", 1), moved(me, "z", -1), opposite]
    )
    links = Links(ssem, rsem)
    xb[me_w, me["x"], me["z"]] = x_ref[...]

    def gather(k, order):
        rows = (pl.ds(128 * k, 64), pl.ds(128 * k + 64, 64))
        whole = pl.ds(128 * k, 128)
        mine = xb.at[me_w, me["x"], me["z"], whole]
        across = links.send(mine, mine, opposite)
        yield
        across.wait_recv()
        sel = {"w": None, "x": me["x"], "z": me["z"]}
        for dim in order:
            def view(i, r, dim=dim, sel=dict(sel)):
                return xb.at[(*ffn_lead({**sel, dim: i}), r)]
            yield from ring_gather(links, me, dim, view, *rows)
            sel[dim] = None

    run(gather(0, "xz"), gather(1, "zx"))

    left_half = lax.broadcasted_iota(jnp.int32, (256, 128), 1) < 64

    def unpack(p, sq):
        w, x, z = lax.div(p, 8), lax.rem(lax.div(p, 2), 4), lax.rem(p, 2) * 2
        a = xb[w, x, z].astype(F32)
        b = xb[w, x, z + 1].astype(F32)
        top = jnp.where(left_half, a, pltpu.roll(b, 64, 1))
        low = jnp.where(left_half, pltpu.roll(a, 64, 1), b)
        at = pl.ds(pl.multiple_of(p * 128, 128), 128)
        xs[0:256, at] = top.astype(BF16)
        xs[256:512, at] = low.astype(BF16)
        return (sq[0] + top * top, sq[1] + low * low)

    zero = jnp.zeros((256, 128), F32)
    squares = lax.fori_loop(0, 16, unpack, (zero, zero))

    for b in range(2):
        mean_sq = jnp.sum(squares[b], axis=1, keepdims=True) * (1.0 / D)
        normed = (
            xs[256 * b : 256 * b + 256].astype(F32) * lax.rsqrt(mean_sq + 1e-06) * gin_ref[...]
        ).astype(BF16)
        hidden = jax.nn.gelu(
            jnp.dot(normed, win_ref[...], preferred_element_type=F32), approximate=True
        ).astype(BF16)
        for n in range(4):
            cols = slice(512 * n, 512 * n + 512)
            part[b, :, :, :, cols] = jnp.dot(
                hidden, wout_ref[:, cols], preferred_element_type=F32
            ).reshape(4, 4, 16, 512)

    def reduce(k, order, far1, near1, far2, near2):
        base = 1024 * k
        low, high = pl.ds(base, 512), pl.ds(base + 512, 512)
        stage = {base: pl.ds(0, 512), base + 512: pl.ds(512, 512)}
        first, second = order
        for dim, far, near, sel, count in (
            (first, far1, near1, {"w": None, second: None}, 8),
            (second, far2, near2, {"w": None, first: me[first]}, 2),
        ):
            def view(i, c, dim=dim, sel=sel):
                return part.at[(*ffn_lead({**sel, dim: i}), ALL, c)]

            lead = (ALL,) * (2 if count == 8 else 1)

            def far_at(n, far=far, lead=lead):
                return lambda c: far.at[(n, *lead)]

            def near_at(n, near=near, lead=lead):
                return lambda c: near.at[(n, *lead, ALL, stage[c.start])]

            def add(i, c, sources, dim=dim, sel=sel, count=count, far=far, near=near):
                def one(t, _):
                    w = lax.rem(t, 2)
                    q = lax.div(t, 2)
                    at = {"w": w, dim: i}
                    other = second if dim == first else first
                    at[other] = q if count == 8 else sel[other]
                    here = (at["w"], at["x"], at["z"], ALL, c)
                    got = (w, q) if count == 8 else (w,)
                    total = part[here]
                    for src in sources:
                        total = total + src(got, c)
                    part[here] = total
                    return 0

                lax.fori_loop(0, count, one, 0)

            def far_val(n, far=far):
                return lambda got, c: far[(n, *got)]

            def near_val(n, near=near):
                return lambda got, c: near[(n, *got, ALL, stage[c.start])]

            class Buffer:
                def __init__(self, ref_at, value):
                    self.ref_at, self.value = ref_at, value

                def __call__(self, *a):
                    return self.ref_at(*a) if len(a) == 1 else self.value(*a)

            yield from ring_reduce(
                links, me, dim, view,
                [Buffer(near_at(n), near_val(n)) for n in range(2)],
                [Buffer(far_at(n), far_val(n)) for n in range(2)],
                low, high, add,
            )
        cols = pl.ds(base, 1024)
        other = 1 - me_w
        got = links.send(
            part.at[other, me["x"], me["z"], :, cols], wrecv.at[:, cols], opposite
        )
        yield
        got.wait_recv()

    run(reduce(0, "zx", far_a, near_a, far_b, near_b), reduce(1, "xz", far_c, near_c, far_d, near_d))

    h = lax.axis_index("hidden")
    inputs = xs[pl.ds(pl.multiple_of(h * 16, 16), 16), :].astype(F32)
    encoded = inputs + (part[me_w, me["x"], me["z"]] + wrecv[...])
    mean_sq = jnp.mean(encoded * encoded, axis=1, keepdims=True)
    lat_ref[...] = (encoded * lax.rsqrt(mean_sq + 1e-06) * gout_ref[...]).astype(BF16)
    links.drain()


def feed_forward(packed, in_gain, w_in, w_out, out_gain):
    vmem = pl.BlockSpec(memory_space=pltpu.VMEM)
    copies = 2 * (1 + 2 * 6) + 2 * (2 * 6 + 1)
    return pl.pallas_call(
        ffn_kernel,
        out_shape=jax.ShapeDtypeStruct((16, D), BF16),
        in_specs=[vmem] * 5,
        out_specs=vmem,
        scratch_shapes=[
            pltpu.VMEM((2, 4, 4, 256, 128), BF16),
            pltpu.VMEM((512, D), BF16),
            pltpu.VMEM((2, 4, 4, 16, D), F32),
        ]
        + [
            pltpu.VMEM((2, *lead, 16, width), F32)
            for _ in range(2)
            for lead in ((2, 4), (2,))
            for width in (512, 1024)
        ]
        + [
            pltpu.VMEM((16, D), F32),
            pltpu.SemaphoreType.DMA((copies,)),
            pltpu.SemaphoreType.DMA((copies,)),
        ],
        compiler_params=pltpu.CompilerParams(
            collective_id=0, has_side_effects=True, vmem_limit_bytes=40 * 2**20
        ),
    )(packed, in_gain, w_in, w_out, out_gain)


ORDERS = ("xyz", "yzx", "zxy")
LAT_COLS = ((0, 384, 384), (768, 384, 256), (1408, 384, 256))
SUM_COLS = ((0, 256, 128), (384, 256, 128), (768, 128, 128))


def lead(sel):
    y = (ALL, ALL) if sel["y"] is None else (lax.rem(sel["y"], 2), lax.div(sel["y"], 2))
    return (*y, *(ALL if sel[d] is None else sel[d] for d in ("x", "z")))


def lead_sizes(dims):
    return tuple(s for d in ("y", "x", "z") if d in dims for s in ((2, 2) if d == "y" else (4,)))


def vocab_kernel(
    lat_ref, table_ref, tail_ref, out_ref, log_ref,
    lat, table, table_t, weights, scores, mixed, sums, stats, factors, got_stats,
    *rest,
):
    *stages, fin, ssem, rsem, load_sem = rest
    me = coords()
    y_lo, y_hi = lax.rem(me["y"], 2), lax.div(me["y"], 2)
    load = pltpu.make_async_copy(
        table_ref.at[pl.ds(0, 1184)], table.at[0, pl.ds(0, 1184)], load_sem
    )
    load.start()
    other_core = device({**me, "c": 1 - me["c"]})
    greet(
        [moved(me, d, s) for d in ("x", "y", "z") for s in (1, -1, 2)] + [other_core]
    )
    links = Links(ssem, rsem)
    lat[y_lo, y_hi, me["x"], me["z"]] = lat_ref[...]

    def gather(order, cols):
        start, n_low, n_high = cols
        low, high = pl.ds(start, n_low), pl.ds(start + n_low, n_high)
        sel = {d: me[d] for d in "xyz"}
        for dim in order:
            def view(i, c, dim=dim, sel=dict(sel)):
                return lat.at[(*lead({**sel, dim: i}), ALL, c)]
            yield from ring_gather(links, me, dim, view, low, high)
            sel[dim] = None

    def swap_table():
        yield
        table[0, 1184:HALF] = tail_ref[...]
        load.wait()
        swap = links.send(table.at[0], table.at[1], other_core)
        for j in range(19):
            if j % 4 == 1:
                yield
            if j == 9:
                swap.wait_recv()
            first = 128 * j
            if first + 128 <= HALF:
                block = table[0, first : first + 128]
            elif first >= HALF:
                block = table[1, first - HALF : first - HALF + 128]
            else:
                block = jnp.concatenate(
                    [table[0, first:HALF], table[1, 0 : first + 128 - HALF]], axis=0
                )
            table_t[:, first : first + 128] = block.T

    run(*(gather(o, c) for o, c in zip(ORDERS, LAT_COLS)), swap_table())

    scale = 5.0 / math.sqrt(D)
    row_id = lax.broadcasted_iota(jnp.int32, (VT, 256), 0)

    def score_block(b, _):
        frames = lat[lax.div(b, 2), lax.rem(b, 2)].reshape(256, D)

        def score_tile(t, top):
            half, lower = lax.div(t, 2), lax.rem(t, 2)
            rows = table[half, pl.ds(pl.multiple_of(lower * VT, VT), VT)]
            s = (
                lax.dot_general(
                    rows, frames, (((1,), (1,)), ((), ())), preferred_element_type=F32
                )
                * scale
            )
            s = jnp.where(row_id < ROWS - lower * VT, s, -1e30)
            scores[t] = s
            return jnp.maximum(top, jnp.max(s, axis=0, keepdims=True))

        top = lax.fori_loop(0, 4, score_tile, jnp.full((1, 256), -1e30, F32))
        lanes = pl.ds(pl.multiple_of(b * 256, 256), 256)

        def weigh(t, total):
            e = jnp.exp(scores[t] - top)
            weights[b, pl.ds(pl.multiple_of(t * VT, VT), VT)] = e.astype(BF16)
            return total + jnp.sum(e, axis=0, keepdims=True)

        total = lax.fori_loop(0, 4, weigh, jnp.zeros((1, 256), F32))
        stats[0, 0:1, lanes] = top
        stats[0, 1:2, lanes] = total
        return 0

    lax.fori_loop(0, 4, score_block, 0)

    def mix(b):
        def tile(n, _):
            rows = pl.ds(pl.multiple_of(n * 512, 512), 512)
            mixed[rows, 256 * b : 256 * b + 256] = jnp.dot(
                table_t[rows, :], weights[b], preferred_element_type=F32
            )
            return 0

        lax.fori_loop(0, 4, tile, 0)

    for phase, dim in enumerate("xyz"):
        copies = [
            links.send(stats.at[phase], got_stats.at[3 * phase + n], moved(me, dim, s))
            for n, s in enumerate((1, -1, 2))
        ]
        mix(phase)
        for copy in copies:
            copy.wait_recv()
        pairs = [stats[phase]] + [got_stats[3 * phase + n] for n in range(3)]
        top = functools.reduce(jnp.maximum, [p[0:1] for p in pairs])
        stats[phase + 1, 0:1] = top
        stats[phase + 1, 1:2] = sum(p[1:2] * jnp.exp(p[0:1] - top) for p in pairs)
    mix(3)

    factors[...] = jnp.exp(stats[0, 0:1] - stats[3, 0:1])

    def rescale(h, _):
        for yl in range(2):
            factor = factors[:, 512 * yl : 512 * yl + 512]
            for j in range(2):
                rows = pl.ds(pl.multiple_of(h * 64 + 32 * j, 32), 32)
                sums[yl, lax.div(h, 16), lax.rem(lax.div(h, 4), 4), lax.rem(h, 4), :, 512 * j : 512 * j + 512] = (
                    mixed[rows, 512 * yl : 512 * yl + 512] * factor
                ).astype(BF16)
        return 0

    lax.fori_loop(0, 32, rescale, 0)

    def reduce(k, order, cols):
        start, n_low, n_high = cols
        low, high = pl.ds(start, n_low), pl.ds(start + n_low, n_high)
        kept = set(order)
        sel = {d: None for d in order}
        for phase, dim in enumerate(order):
            kept = kept - {dim}
            sizes = lead_sizes(kept)
            far_low, far_high, near = stages[(k * 3 + phase) * 3 : (k * 3 + phase) * 3 + 3]
            count = math.prod(sizes)
            all_lead = (ALL,) * len(sizes)

            def inner(c, start=start):
                return pl.ds(c.start - start, c.size)

            def view(i, c, dim=dim, sel=dict(sel)):
                return sums.at[(*lead({**sel, dim: i}), ALL, c)]

            class Buffer:
                def __init__(self, ref, n, cut):
                    self.ref, self.n, self.cut = ref, n, cut

                def __call__(self, c, got=all_lead):
                    at = (*self.n, *got)
                    return self.ref.at[(*at, ALL, inner(c))] if self.cut else self.ref.at[at] if at else self.ref

                def value(self, c, got):
                    at = (*self.n, *got)
                    return self.ref[(*at, ALL, inner(c))] if self.cut else self.ref[(*at, ALL, ALL)]

            def add(i, c, sources, dim=dim, sel=dict(sel), kept=kept, sizes=sizes, count=count):
                def one(t, _):
                    got, rest_t = [], t
                    for s in reversed(sizes):
                        got.insert(0, lax.rem(rest_t, s))
                        rest_t = lax.div(rest_t, s)
                    got = tuple(got)
                    at = {**sel, dim: i}
                    left = list(got)
                    here = []
                    for d in ("y", "x", "z"):
                        n = 2 if d == "y" else 1
                        if d in kept:
                            here += left[:n]
                            left = left[n:]
                        elif d == "y":
                            here += [lax.rem(at["y"], 2), lax.div(at["y"], 2)]
                        else:
                            here.append(at[d])
                    here = (*here, ALL, c)
                    total = sums[here].astype(F32)
                    for src in sources:
                        total = total + src.value(c, got).astype(F32)
                    if kept or len(sources) == 1:
                        sums[here] = total.astype(BF16)
                    else:
                        fin[:, c] = total
                    return 0

                if count == 1:
                    one(0, 0)
                else:
                    lax.fori_loop(0, count, one, 0)

            yield from ring_reduce(
                links, me, dim, view,
                [Buffer(near, (0,), True), Buffer(near, (1,), True)],
                [Buffer(far_low, (), False), Buffer(far_high, (), False)],
                low, high, add,
            )
            sel[dim] = me[dim]

    run(*(reduce(k, o, c) for k, (o, c) in enumerate(zip(ORDERS, SUM_COLS))))

    lanes = pl.ds(pl.multiple_of(y_lo * 512, 512), 512)
    top, total = stats[3, 0:1, lanes], stats[3, 1:2, lanes]
    for j in range(2):
        out_ref[32 * j : 32 * j + 32, :] = (fin[:, 512 * j : 512 * j + 512] / total).astype(BF16)
    log_ref[...] = top + jnp.log(total)
    links.drain()


def vocabulary(latent, table, tail):
    vmem = pl.BlockSpec(memory_space=pltpu.VMEM)
    copies = 3 * 3 * 6 * 2 + 9 + 1
    stages = []
    for order, (start, n_low, n_high) in zip(ORDERS, SUM_COLS):
        for phase in range(3):
            sizes = lead_sizes(order[phase + 1 :])
            stages += [
                pltpu.VMEM((*sizes, 32, n_low), BF16),
                pltpu.VMEM((*sizes, 32, n_high), BF16),
                pltpu.VMEM((2, *sizes, 32, n_low + n_high), BF16),
            ]
    return pl.pallas_call(
        vocab_kernel,
        out_shape=(
            jax.ShapeDtypeStruct((64, 512), BF16),
            jax.ShapeDtypeStruct((1, 512), F32),
        ),
        in_specs=[vmem, pl.BlockSpec(memory_space=pl.ANY), vmem],
        out_specs=(vmem, vmem),
        scratch_shapes=[
            pltpu.VMEM((2, 2, 4, 4, 16, D), BF16),
            pltpu.VMEM((2, HALF, D), BF16),
            pltpu.VMEM((D, VP), BF16),
            pltpu.VMEM((4, VP, 256), BF16),
            pltpu.VMEM((4, VT, 256), F32),
            pltpu.VMEM((D, 1024), F32),
            pltpu.VMEM((2, 2, 4, 4, 32, 1024), BF16),
            pltpu.VMEM((4, 8, 1024), F32),
            pltpu.VMEM((1, 1024), F32),
            pltpu.VMEM((9, 8, 1024), F32),
            *stages,
            pltpu.VMEM((32, 1024), F32),
            pltpu.SemaphoreType.DMA((copies,)),
            pltpu.SemaphoreType.DMA((copies,)),
            pltpu.SemaphoreType.DMA,
        ],
        compiler_params=pltpu.CompilerParams(
            collective_id=1, has_side_effects=True, vmem_limit_bytes=60 * 2**20
        ),
    )(latent, table, tail)


def shards(frames_in, in_gain, w_in, w_out, out_gain, table):
    packed = jnp.concatenate([frames_in[:256], frames_in[256:]], axis=1)
    tail = jnp.pad(table[1184:], ((0, HALF - ROWS), (0, 0)))
    latent = feed_forward(packed, in_gain[None], w_in, w_out, out_gain[None])
    mixed, log_total = vocabulary(latent, table, tail)
    return (mixed.T, log_total.reshape(512))


def solution(mesh):
    placed = (
        P("frames", "hidden"),
        P(),
        P(None, "hidden"),
        P("hidden", None),
        P(),
        P(("frames", "hidden"), None),
    )
    return jax.shard_map(
        shards,
        mesh=mesh,
        in_specs=placed,
        out_specs=(P("frames", "hidden"), P("frames")),
        check_vma=False,
    )
```

time: 814 us -> 164 us (0.20)
  waiting for transfers between devices: 533 us -> 0 us
  blocking collectives: 185 us -> 0 us
  Pallas kernels: 0 us -> 154 us
  matrix products: 41.5 us -> 0 us
  local copies, waits for them, and re-layouts: 28.3 us -> 9.63 us
  between operations: 15.3 us -> 0.68 us
  other arithmetic: 9.28 us -> 0.1 us
    psum x1 -> x0, waiting for transfers between devices: 363 us -> none  [shards(): encoded = lax.psum(ffn_partial, 'hidden') + inputs]
    pallas_call x0 -> x2, Pallas kernels: none -> 154 us  [the longest x1 92.6 us: vocabulary(): pl.pallas_call(vocab_kernel, out_shape=(jax.ShapeDtypeStruct((64, 512), B...]
    pmax x1 -> x0, blocking collectives: 96 us -> none  [shards(): highest = lax.pmax(local_top, 'hidden')]
    unnamed x5 -> x0, waiting for transfers between devices: 93.9 us -> none
    psum x1 -> x0, blocking collectives: 88.9 us -> none  [shards(): row_total = lax.psum(jnp.sum(exponent, axis=0), 'hidden')]
    all_gather x2 -> x0, waiting for transfers between devices: 76.6 us -> none  [the longest x1 76.6 us: shards(): full_rows = lax.all_gather(frames_in, 'hidden', axis=1, tiled=True)]
    dot_general x3 -> x0, matrix products: 41.5 us -> none  [the longest x1 18.6 us: shards(): lax.dot_general(vocab_rows, weights, contract_rows, preferred_element_typ...]
    unnamed x12 -> x14, local copies, waits for them, and re-layouts: 25.4 us -> 7.42 us
  transfers between devices with their start and end apart: 4 -> 0, of which waited for: 3 -> 0; matrix products, arithmetic and copies ran while one was open for 1% -> 0% of each run, Pallas kernels for 0% -> 0%
where the time goes in v1:
time: 164 us
  Pallas kernels  154 us (94%)
  local copies, waits for them, and re-layouts  9.63 us (6%)
    pallas_call x1, Pallas kernels, vocabulary(): pl.pallas_call(vocab_kernel, out_shape=(jax.ShapeDtypeStruct((64, 512), B...  92.6 us
    pallas_call x1, Pallas kernels, feed_forward(): pl.pallas_call(ffn_kernel, out_shape=jax.ShapeDtypeStruct((16, D), BF16),...  60.9 us
    unnamed x14, local copies, waits for them, and re-layouts  7.42 us

profile of v1, /device:TPU:0, one launch (start us, length us, event | category | flops | bytes accessed | tf_op | source)
XLA Modules:
  0.0 164.0 jit_solution(13829781926261962379)
XLA Ops:
  0.6 0.8 slice.11
  1.4 0.8 fusion
  2.2 0.1 copy.10
  2.3 0.1 copy.11
  2.4 0.1 pad_maximum_fusion.x_ref
  2.5 0.0 copy-start
  2.5 1.2 copy-done
  3.7 0.0 copy-start.1
  3.8 1.2 copy-done.1
  5.0 0.0 copy-start.3
  5.0 0.7 copy-done.3
  5.7 0.0 copy-start.4
  5.7 0.7 copy-done.4
  6.4 60.9 %shard_map.77.lat_ref = bf16[16,2048]{1,0:T(8,128)(2,1)S(1)} custom-call(bf16[256,128]{1,0:T(8,128)(2,1)S(1)} %pad_maximum_fusion.x_ref, f32[1,2048]{1,0:T(1,128)S(1)} %bitcast.4, bf16[2048,256]{1,0:T(8,128)(2,1)S(1)} %copy-done, bf16[256,2048]{1,0:T(8,128)(2,1)S(1)} %copy-done.1, f32[1,2048]{1,0:T(1,128)S(1)} %bitcast.5), custom_call_target="tpu_custom_call" | custom-call | tf_op jit(solution)/shard_map/pallas_call | solution.py:268
  67.3 0.0 copy-start.2
  67.3 0.6 copy-done.2
  67.9 0.7 pad.4.tail_ref
  68.6 92.6 %shard_map.78 = (bf16[64,512]{1,0:T(8,128)(2,1)}, f32[1,512]{1,0:T(1,128)}) custom-call(bf16[16,2048]{1,0:T(8,128)(2,1)} %copy-done.2, bf16[1187,2048]{1,0:T(8,128)(2,1)} %table_ref.1, bf16[32,2048]{1,0:T(8,128)(2,1)} %pad.4.tail_ref), custom_call_target="tpu_custom_call" | custom-call | tf_op jit(solution)/shard_map/pallas_call | solution.py:527
  161.3 1.5 copy.14
  162.7 1.3 copy.15
Async XLA Ops:
  2.5 1.2 copy-start
  3.7 1.2 copy-start.1
  5.0 0.7 copy-start.3
  5.7 0.7 copy-start.4
  67.3 0.6 copy-start.2

commit v2 on v0

v2 whole, which is shorter than its diff:
```python
import functools
import math

import jax
import jax.numpy as jnp
from jax import lax
from jax.experimental import pallas as pl
from jax.experimental.pallas import tpu as pltpu
from jax.sharding import PartitionSpec as P

MESH = pl.DeviceIdType.MESH
D = 2048
ROWS = 1187
TAIL = 1168
REST = 32
AGAIN = REST - (ROWS - TAIL)
WIDE = 1280
F32 = jnp.float32
BF16 = jnp.bfloat16
ALL = slice(None)


def coords():
    f = lax.axis_index("frames")
    h = lax.axis_index("hidden")
    return {
        "x": lax.rem(lax.div(h, 4), 4),
        "y": lax.div(h, 16) * 2 + lax.div(f, 2),
        "z": lax.rem(h, 4),
        "c": lax.rem(f, 2),
    }


def device(at):
    return (
        lax.rem(at["y"], 2) * 2 + at["c"],
        lax.div(at["y"], 2) * 16 + at["x"] * 4 + at["z"],
    )


def moved(me, dim, by):
    return device({**me, dim: lax.rem(me[dim] + by + 4, 4)})


class Links:
    def __init__(self, send_sems, recv_sems):
        self.send_sems, self.recv_sems = send_sems, recv_sems
        self.count, self.flying = 0, []

    def send(self, src, dst, to):
        copy = pltpu.make_async_remote_copy(
            src_ref=src,
            dst_ref=dst,
            send_sem=self.send_sems.at[self.count],
            recv_sem=self.recv_sems.at[self.count],
            device_id=to,
            device_id_type=MESH,
        )
        copy.start()
        self.count += 1
        self.flying.append(copy)
        return copy

    def drain(self):
        for copy in self.flying:
            copy.wait_send()
        self.flying = []


def run(*streams):
    streams = list(streams)
    while streams:
        for stream in list(streams):
            try:
                next(stream)
            except StopIteration:
                streams.remove(stream)


def gather_stream(links, me, buf, order, direct):
    for k, dim in enumerate(order):
        fixed = tuple(me[d] for d in reversed(order[k + 1 :]))
        i = me[dim]
        right, left = moved(me, dim, 1), moved(me, dim, -1)
        before, after = lax.rem(i + 3, 4), lax.rem(i + 1, 4)

        def go(j, part, to, fixed=fixed):
            cut = () if part is None else (slice(2 * part, 2 * part + 2),)
            block = buf.at[(*fixed, j, *cut)]
            return links.send(block, block, to)

        if direct[k]:
            copies = [go(i, None, to) for to in (moved(me, dim, 2), right, left)]
            yield
            for copy in copies:
                copy.wait_recv()
            continue
        r_low, l_high = go(i, 0, right), go(i, 1, left)
        r_high, l_low = go(i, 1, right), go(i, 0, left)
        yield
        r_low.wait_recv()
        r_far = go(before, 0, right)
        l_high.wait_recv()
        l_far = go(after, 1, left)
        yield
        for copy in (r_high, l_low, r_far, l_far):
            copy.wait_recv()


def add_stream(links, me, buf, stages, order, direct, result):
    for k, dim in enumerate(order):
        fixed = tuple(me[d] for d in order[:k])
        left_dims = len(order) - 1 - k
        i = me[dim]
        right, left = moved(me, dim, 1), moved(me, dim, -1)
        before, after, across = lax.rem(i + 3, 4), lax.rem(i + 1, 4), lax.rem(i + 2, 4)

        def view(j, part, fixed=fixed):
            cut = () if part is None else (slice(2 * part, 2 * part + 2),)
            return buf.at[(*fixed, j, *cut)]

        def add(j, at, sources, fixed=fixed, left_dims=left_dims):
            total = buf[(*fixed, j, *at)].astype(F32)
            for ref, lead in sources:
                total = total + ref[lead].astype(F32)
            if left_dims == 0:
                result(total)
            else:
                buf[(*fixed, j, *at)] = total.astype(buf.dtype)

        if direct[k]:
            (near,) = stages[k]
            copies = [
                links.send(view(j, None), near.at[n], to)
                for n, (j, to) in enumerate(
                    ((across, moved(me, dim, 2)), (after, right), (before, left))
                )
            ]
            yield
            for copy in copies:
                copy.wait_recv()
            add(i, () if left_dims else (ALL, ALL), [(near, (n,)) for n in range(3)])
            continue
        far, near = stages[k]
        r_far = links.send(view(across, 0), far.at[0], right)
        l_far = links.send(view(across, 1), far.at[1], left)
        r_high = links.send(view(after, 1), near.at[0, 2:4], right)
        l_low = links.send(view(before, 0), near.at[1, 0:2], left)
        yield
        r_far.wait_recv()
        for t in range(2):
            add(after, (t,), [(far, (0, t))])
        r_low = links.send(view(after, 0), near.at[0, 0:2], right)
        l_far.wait_recv()
        for t in range(2):
            add(before, (2 + t,), [(far, (1, t))])
        l_high = links.send(view(before, 1), near.at[1, 2:4], left)
        yield
        r_high.wait_recv()
        l_high.wait_recv()
        for t in (2, 3):
            add(i, (t,), [(near, (0, t)), (near, (1, t))])
        l_low.wait_recv()
        r_low.wait_recv()
        for t in (0, 1):
            add(i, (t,), [(near, (0, t)), (near, (1, t))])


def stage_shapes(direct, rows, width, dtype):
    shapes = []
    for k, straight in enumerate(direct):
        block = (4,) * (len(direct) - 1 - k)
        if not straight:
            shapes.append(pltpu.VMEM((2, 2, *block[1:], rows, width), dtype))
        shapes.append(pltpu.VMEM((3 if straight else 2, *block, rows, width), dtype))
    return shapes


def by_phase(direct, refs):
    refs = iter(refs)
    return [(next(refs),) if straight else (next(refs), next(refs)) for straight in direct]


def greet(peers):
    barrier = pltpu.get_barrier_semaphore()
    for peer in peers:
        pl.semaphore_signal(barrier, inc=1, device_id=peer, device_id_type=MESH)
    pl.semaphore_wait(barrier, len(peers))


FFN_ORDERS = ("xz", "zx")
FFN_GATHER, FFN_ADD = (True, True), (False, True)
GATHER, ADD = (True, True, False), (False, True, True)


def feed_forward(links, me, other_core, x_ref, gin_ref, gout_ref, w_hbm, loads, refs, beside):
    xp, xs, win, wout, *refs = refs
    gathered, partial = refs[0:2], refs[2:4]
    n = (len(refs) - 4) // 2
    stages = [by_phase(FFN_ADD, refs[4 + n * k : 4 + n * k + n]) for k in range(2)]
    y_lo, half = lax.rem(me["y"], 2), lax.div(me["y"], 2)
    opposite = moved(me, "y", 2)
    cross = moved(me, "y", 2 * y_lo - 1)
    beside_y = moved(me, "y", 1 - 2 * y_lo)
    mine = y_lo * 2 + me["c"]

    def exchange_weights():
        theirs = (1 - y_lo) * 2 + me["c"]
        jobs = []
        for ref, hbm, rows, n in ((win, w_hbm[0], 512, 256), (wout, w_hbm[1], 64, 32)):
            for at in range(0, rows, n):
                own = pl.ds(pl.multiple_of(mine * rows + at, n), n)
                next_to = pl.ds(pl.multiple_of(theirs * rows + at, n), n)
                jobs.append((ref, hbm, own, next_to))

        def start(job):
            ref, hbm, own, next_to = job
            return links.send(hbm.at[next_to], ref.at[1, next_to], cross)

        got = [start(job) for job in jobs]
        passed, last = [], []

        def hand_over(n):
            ref, _, _, next_to = jobs[n]
            passed[n].wait_recv()
            last.append(links.send(ref.at[1, next_to], ref.at[1, next_to], other_core))

        for n, (ref, _, own, _) in enumerate(jobs):
            yield
            got[n].wait_recv()
            passed.append(links.send(ref.at[1, own], ref.at[1, own], beside_y))
            last.append(links.send(ref.at[1, own], ref.at[1, own], other_core))
            if n >= 1:
                hand_over(n - 1)
        yield
        hand_over(len(jobs) - 1)
        yield
        for copy in last:
            copy.wait_recv()

    lanes = lax.broadcasted_iota(jnp.int32, (256, 128), 1) < 64

    def exchange_frames():
        xp[half] = jnp.concatenate([x_ref[:, 0:256], x_ref[:, 256:512]], axis=0).T
        got = links.send(xp.at[half], xp.at[half], opposite)
        yield
        got.wait_recv()
        p = [xp[0].astype(F32), xp[1].astype(F32)]
        r = [pltpu.roll(v, 64, 1) for v in p]
        first = half == 0
        block = jnp.where(
            lanes, jnp.where(first, p[0], r[0]), jnp.where(first, r[1], p[1])
        ).astype(BF16)
        for k, order in enumerate(FFN_ORDERS):
            gathered[k][me[order[1]], me[order[0]]] = block[128 * k : 128 * k + 128]
        streams = [gather_stream(links, me, gathered[k], o, FFN_GATHER) for k, o in enumerate(FFN_ORDERS)]
        while streams:
            for stream in list(streams):
                try:
                    next(stream)
                except StopIteration:
                    streams.remove(stream)
            if streams:
                yield

    run(
        exchange_frames(),
        exchange_weights(),
        *beside,
    )
    few = lax.broadcasted_iota(jnp.int32, (128, 128), 1) < 64

    def unpack(p, squares):
        x, z = lax.div(p, 2), lax.rem(p, 2) * 2
        at = pl.multiple_of(p * 128, 128)
        sums = []
        for k in range(2):
            ref = gathered[k]
            a, b = (ref[z, x], ref[z + 1, x]) if k == 0 else (ref[x, z], ref[x, z + 1])
            a, b = a.astype(F32), b.astype(F32)
            rows = slice(128 * k, 128 * k + 128)
            top = jnp.where(few, a, pltpu.roll(b, 64, 1))
            low = jnp.where(few, pltpu.roll(a, 64, 1), b)
            xs[rows, pl.ds(at, 128)] = top.astype(BF16)
            xs[rows, pl.ds(at + 1024, 128)] = low.astype(BF16)
            sums.append(squares[k] + a * a + b * b)
        return tuple(sums)

    squares = lax.fori_loop(0, 8, unpack, (jnp.zeros((128, 128), F32),) * 2)
    mean_sq = jnp.sum(jnp.concatenate(squares, axis=0), axis=1, keepdims=True) * (1.0 / D)
    normed = (xs[...].astype(F32) * lax.rsqrt(mean_sq + 1e-06) * gin_ref[...]).astype(BF16)
    for load in loads:
        load.wait()
    hidden = [
        jax.nn.gelu(
            jnp.dot(normed, win[w], preferred_element_type=F32), approximate=True
        ).astype(BF16)
        for w in range(2)
    ]
    for k, order in enumerate(FFN_ORDERS):
        for part in range(2):
            cols = slice(1024 * k + 512 * part, 1024 * k + 512 * part + 512)
            block = jnp.dot(hidden[0], wout[0, :, cols], preferred_element_type=F32) + jnp.dot(
                hidden[1], wout[1, :, cols], preferred_element_type=F32
            )
            for t in range(16):
                at = (t // 4, t % 4) if order == "xz" else (t % 4, t // 4)
                partial[k][(*at, ALL, slice(512 * part, 512 * part + 512))] = block[16 * t : 16 * t + 16]
    found = {}
    run(
        *(
            add_stream(
                links, me, partial[k], stages[k], order, FFN_ADD,
                lambda value, k=k: found.update({k: value}),
            )
            for k, order in enumerate(FFN_ORDERS)
        )
    )
    row = pl.ds(pl.multiple_of(16 * (4 * me["x"] + me["z"]), 16), 16)
    total = jnp.concatenate([found[0], found[1]], axis=1)
    encoded = xs[row, :].astype(F32) + total
    mean_sq = jnp.mean(encoded * encoded, axis=1, keepdims=True)
    return (encoded * lax.rsqrt(mean_sq + 1e-06) * gout_ref[...]).astype(BF16)


FFN_SCRATCH = (
    [
        pltpu.VMEM((2, 256, 128), BF16),
        pltpu.VMEM((256, D), BF16),
        pltpu.VMEM((2, D, 256), BF16),
        pltpu.VMEM((2, 256, D), BF16),
    ]
    + [pltpu.VMEM((4, 4, 128, 128), BF16)] * 2
    + [pltpu.VMEM((4, 4, 16, 1024), F32)] * 2
    + stage_shapes(FFN_ADD, 16, 1024, F32) * 2
)
FFN_COPIES = 1 + 2 * (3 + 3) + 4 * 4 + 2 * (6 + 3)


ORDERS = ("xyz", "yzx", "zxy")
SPLITS = ((0, 384), (384, 384), (768, 256))


def kernel(
    x_ref, gin_ref, gout_ref, win_hbm, wout_hbm, table_hbm, tail_ref, out_ref, log_ref,
    turned, pieces, lat, scores, weights, stats, got_stats, factors, fin,
    *rest,
):
    ffn_refs, rest = rest[: len(FFN_SCRATCH)], rest[len(FFN_SCRATCH) :]
    buffers = [rest[0:3], rest[3:6]]
    *stages, ssem, rsem, load_sem = rest[6:]
    me = coords()
    y_lo, y_hi = lax.rem(me["y"], 2), lax.div(me["y"], 2)
    load_in = pltpu.make_async_copy(win_hbm, ffn_refs[2].at[0], load_sem.at[0])
    load_out = pltpu.make_async_copy(wout_hbm, ffn_refs[3].at[0], load_sem.at[1])
    load_in.start()
    load_out.start()

    def load_piece(p):
        n = min(256, TAIL - 256 * p)
        copy = pltpu.make_async_copy(
            table_hbm.at[pl.ds(256 * p, n)], pieces.at[p % 2, pl.ds(0, n)], load_sem.at[2 + p]
        )
        copy.start()
        return copy

    coming = [load_piece(0), load_piece(1)]
    other_core = device({**me, "c": 1 - me["c"]})
    greet([moved(me, d, s) for d in ("x", "y", "z") for s in (1, -1, 2)] + [other_core])
    links = Links(ssem, rsem)
    swaps = []

    def turn_table():
        yield
        for p in range(5):
            coming[p].wait()
            if p == 4:
                pieces[0, TAIL - 1024 : TAIL + REST - 1024] = tail_ref[...]
                pieces[0, TAIL + REST - 1024 : 256] = jnp.zeros((WIDE - TAIL - REST, D), BF16)
            for q in range(2):
                block = pieces[p % 2, 128 * q : 128 * q + 128]
                at = 256 * p + 128 * q
                turned[0, :, at : at + 128] = block.T
            if p + 2 < 5:
                coming.append(load_piece(p + 2))
            if p < 4:
                yield
        swaps.append(links.send(turned.at[0], turned.at[1], other_core))

    latent = feed_forward(
        links, me, other_core, x_ref, gin_ref, gout_ref, (win_hbm, wout_hbm), (load_in, load_out),
        ffn_refs, (turn_table(),),
    )
    for s in range(2):
        for buf, order, (start, width) in zip(buffers[s], ORDERS, SPLITS):
            at = 1024 * s + start
            buf[tuple(me[d] for d in reversed(order))] = latent[:, at : at + width]

    done = set()

    def then(stream, *keys):
        yield from stream
        done.update(keys)

    def after(keys, stream):
        while not set(keys) <= done:
            yield
        yield from stream

    scale = 5.0 / math.sqrt(D)

    def collect(s):
        def block(t, _):
            at = {"y": lax.div(t, 16), "x": lax.rem(lax.div(t, 4), 4), "z": lax.rem(t, 4)}
            to = (lax.rem(at["y"], 2), lax.div(at["y"], 2), at["x"], at["z"])
            for buf, order, (start, width) in zip(buffers[s], ORDERS, SPLITS):
                cols = slice(1024 * s + start, 1024 * s + start + width)
                lat[(*to, ALL, cols)] = buf[tuple(at[d] for d in reversed(order))]
            return 0

        lax.fori_loop(0, 64, block, 0)

    def score(s, g):
        frames = lat[:, g, :, :, :, 1024 * s : 1024 * s + 1024].reshape(512, 1024)

        def tile(t, _):
            half, n = lax.div(t, 5), lax.rem(t, 5)
            cols = pl.ds(pl.multiple_of(n * 256, 256), 256)
            at = pl.ds(pl.multiple_of(t * 256, 256), 256)
            product = jnp.dot(
                frames, turned[half, 1024 * s : 1024 * s + 1024, cols], preferred_element_type=F32
            )
            scores[g, :, at] = product if s == 0 else scores[g, :, at] + product
            return 0

        lax.fori_loop(0, 10, tile, 0)

    lane_id = lax.broadcasted_iota(jnp.int32, (1, 2 * WIDE), 1)
    place = lax.rem(lane_id, WIDE)
    real = (place < TAIL) | ((place >= TAIL + AGAIN) & (place < TAIL + REST))

    def softmax(g):
        def rows(r, _):
            at = pl.ds(pl.multiple_of(r * 32, 32), 32)
            s = jnp.where(real, scores[g, at, :] * scale, -1e30)
            top = jnp.max(s, axis=1, keepdims=True)
            e = jnp.exp(s - top)
            weights[g, at, :] = e.astype(BF16)
            factors[0, at, :] = jnp.broadcast_to(top, (32, 128))
            factors[1, at, :] = jnp.broadcast_to(jnp.sum(e, axis=1, keepdims=True), (32, 128))
            return 0

        lax.fori_loop(0, 16, rows, 0)
        stats[g, 0, 0:1] = factors[0].T[0:1]
        stats[g, 0, 1:2] = factors[1].T[0:1]

    def share_stats(g):
        for phase, dim in enumerate("xyz"):
            copies = [
                links.send(stats.at[g, phase], got_stats.at[g, 3 * phase + n], moved(me, dim, s))
                for n, s in enumerate((1, -1, 2))
            ]
            yield
            for copy in copies:
                copy.wait_recv()
            pairs = [stats[g, phase]] + [got_stats[g, 3 * phase + n] for n in range(3)]
            top = functools.reduce(jnp.maximum, [p[0:1] for p in pairs])
            stats[g, phase + 1, 0:1] = top
            stats[g, phase + 1, 1:2] = sum(p[1:2] * jnp.exp(p[0:1] - top) for p in pairs)

    def mix(g, n):
        rows = slice(512 * n, 512 * n + 512)
        dims = (((1,), (1,)), ((), ()))

        def tile(q, _):
            frames = pl.ds(pl.multiple_of(q * 256, 256), 256)
            total = lax.dot_general(
                turned[0, rows, :], weights[g, frames, 0:WIDE], dims, preferred_element_type=F32
            ) + lax.dot_general(
                turned[1, rows, :], weights[g, frames, WIDE:], dims, preferred_element_type=F32
            )
            scores[g, :, pl.ds(pl.multiple_of(512 * n + q * 256, 256), 256)] = total
            return 0

        lax.fori_loop(0, 2, tile, 0)

    def rescale(g):
        factor = jnp.exp(stats[g, 0, 0:1] - stats[g, 3, 0:1])

        def block(h8, _):
            for n in range(4):
                h = 8 * n + h8
                y_up, x, z = lax.div(h, 16), lax.rem(lax.div(h, 4), 4), lax.rem(h, 4)
                for yl in range(2):
                    at = {"x": x, "y": 2 * y_up + yl, "z": z}
                    for buf, order, (start, width) in zip(buffers[g], ORDERS, SPLITS):
                        for c in range(width // 128):
                            unit = start // 128 + c
                            lane = 256 * yl + 128 * (unit % 2)
                            rows = pl.ds(pl.multiple_of(h8 * 64 + 16 * (unit // 2), 16), 16)
                            value = scores[g, rows, 512 * n + lane : 512 * n + lane + 128]
                            buf[(*(at[d] for d in order), ALL, slice(128 * c, 128 * c + 128))] = (
                                value * factor[:, lane : lane + 128]
                            ).astype(BF16)
            return 0

        lax.fori_loop(0, 8, block, 0)

    def wait_for(*keys):
        while not set(keys) <= done:
            yield

    def compute():
        yield from wait_for(*(f"lat0{k}" for k in range(3)))
        swaps[0].wait_recv()
        collect(0)
        for g in range(2):
            score(0, g)
            yield
        yield from wait_for(*(f"lat1{k}" for k in range(3)))
        collect(1)
        links.drain()
        for g in range(2):
            score(1, g)
            softmax(g)
            done.add(f"local{g}")
            yield
        for n in range(4):
            mix(0, n)
            if n % 2:
                yield
        yield from wait_for("stats0")
        rescale(0)
        done.add("sums0")
        yield
        for n in range(4):
            mix(1, n)
        yield from wait_for("stats1")
        rescale(1)
        done.add("sums1")

    def final():
        for g in range(2):
            yield from wait_for(*(f"out{g}{k}" for k in range(3)))
            lanes = pl.ds(pl.multiple_of(y_lo * 256, 256), 256)
            top, total = stats[g, 3, 0:1, lanes], stats[g, 3, 1:2, lanes]
            for j in range(4):
                out_ref[16 * j : 16 * j + 16, 256 * g : 256 * g + 256] = (
                    fin[g, :, 256 * j : 256 * j + 256] / total
                ).astype(BF16)
            log_ref[:, 256 * g : 256 * g + 256] = top + jnp.log(total)

    def delayed(stream, rounds):
        for _ in range(rounds):
            yield
        yield from stream

    streams = [
        then(delayed(gather_stream(links, me, buffers[s][k], o, GATHER), 2 * s), f"lat{s}{k}")
        for s in range(2)
        for k, o in enumerate(ORDERS)
    ]
    streams.append(compute())
    streams += [then(after([f"local{g}"], share_stats(g)), f"stats{g}") for g in range(2)]
    for g in range(2):
        for k, (o, (start, width)) in enumerate(zip(ORDERS, SPLITS)):
            def result(value, g=g, start=start, width=width):
                fin[g, :, start : start + width] = value

            n = len(stages) // 6
            at = n * (3 * g + k)
            stream = add_stream(
                links, me, buffers[g][k], by_phase(ADD, stages[at : at + n]), o, ADD, result
            )
            streams.append(then(after([f"sums{g}"], stream), f"out{g}{k}"))
    streams.append(final())
    run(*streams)
    links.drain()


def fused(frames_in, in_gain, out_gain, w_in, w_out, table, tail):
    vmem = pl.BlockSpec(memory_space=pltpu.VMEM)
    hbm = pl.BlockSpec(memory_space=pl.ANY)
    copies = FFN_COPIES + 1 + 2 * 9 + 2 * 3 * 2 * 12
    buffers, stages = [], []
    for _ in range(2):
        for _, width in SPLITS:
            buffers.append(pltpu.VMEM((4, 4, 4, 16, width), BF16))
            stages += stage_shapes(ADD, 16, width, BF16)
    return pl.pallas_call(
        kernel,
        out_shape=(
            jax.ShapeDtypeStruct((64, 512), BF16),
            jax.ShapeDtypeStruct((1, 512), F32),
        ),
        in_specs=[vmem] * 3 + [hbm] * 3 + [vmem],
        out_specs=(vmem, vmem),
        scratch_shapes=[
            pltpu.VMEM((2, D, WIDE), BF16),
            pltpu.VMEM((2, 256, D), BF16),
            pltpu.VMEM((2, 2, 4, 4, 16, D), BF16),
            pltpu.VMEM((2, 512, 2 * WIDE), F32),
            pltpu.VMEM((2, 512, 2 * WIDE), BF16),
            pltpu.VMEM((2, 4, 8, 512), F32),
            pltpu.VMEM((2, 9, 8, 512), F32),
            pltpu.VMEM((2, 512, 128), F32),
            pltpu.VMEM((2, 16, 1024), F32),
            *FFN_SCRATCH,
            *buffers,
            *stages,
            pltpu.SemaphoreType.DMA((copies,)),
            pltpu.SemaphoreType.DMA((copies,)),
            pltpu.SemaphoreType.DMA((7,)),
        ],
        compiler_params=pltpu.CompilerParams(
            collective_id=0, has_side_effects=True, vmem_limit_bytes=61 * 2**20
        ),
    )(frames_in, in_gain, out_gain, w_in, w_out, table, tail)


def shards(frames_in, in_gain, w_in, w_out, out_gain, table):
    tail = table[ROWS - REST :]
    mixed, log_total = fused(frames_in.T, in_gain[None], out_gain[None], w_in, w_out, table, tail)
    return (mixed.T, log_total.reshape(512))


def solution(mesh):
    placed = (
        P("frames", "hidden"),
        P(),
        P(None, "hidden"),
        P("hidden", None),
        P(),
        P(("frames", "hidden"), None),
    )
    return jax.shard_map(
        shards,
        mesh=mesh,
        in_specs=placed,
        out_specs=(P("frames", "hidden"), P("frames")),
        check_vma=False,
    )
```

time: 814 us -> 145 us (0.18)
  waiting for transfers between devices: 533 us -> 0 us
  blocking collectives: 185 us -> 0 us
  Pallas kernels: 0 us -> 140 us
  matrix products: 41.5 us -> 0 us
  local copies, waits for them, and re-layouts: 28.3 us -> 4.31 us
  between operations: 15.3 us -> 0.64 us
  other arithmetic: 9.28 us -> 0 us
    psum x1 -> x0, waiting for transfers between devices: 363 us -> none  [shards(): encoded = lax.psum(ffn_partial, 'hidden') + inputs]
    pallas_call x0 -> x1, Pallas kernels: none -> 140 us  [fused(): pl.pallas_call(kernel, out_shape=(jax.ShapeDtypeStruct((64, 512), BF16),...]
    pmax x1 -> x0, blocking collectives: 96 us -> none  [shards(): highest = lax.pmax(local_top, 'hidden')]
    unnamed x5 -> x0, waiting for transfers between devices: 93.9 us -> none
    psum x1 -> x0, blocking collectives: 88.9 us -> none  [shards(): row_total = lax.psum(jnp.sum(exponent, axis=0), 'hidden')]
    all_gather x2 -> x0, waiting for transfers between devices: 76.6 us -> none  [the longest x1 76.6 us: shards(): full_rows = lax.all_gather(frames_in, 'hidden', axis=1, tiled=True)]
    dot_general x3 -> x0, matrix products: 41.5 us -> none  [the longest x1 18.6 us: shards(): lax.dot_general(vocab_rows, weights, contract_rows, preferred_element_typ...]
    unnamed x12 -> x2, local copies, waits for them, and re-layouts: 25.4 us -> 2.71 us
  transfers between devices with their start and end apart: 4 -> 0, of which waited for: 3 -> 0; matrix products, arithmetic and copies ran while one was open for 1% -> 0% of each run, Pallas kernels for 0% -> 0%
where the time goes in v2:
time: 145 us
  Pallas kernels  140 us (97%)
  local copies, waits for them, and re-layouts  4.31 us (3%)
    pallas_call x1, Pallas kernels, fused(): pl.pallas_call(kernel, out_shape=(jax.ShapeDtypeStruct((64, 512), BF16),...  140 us

profile of v2, /device:TPU:0, one launch (start us, length us, event | category | flops | bytes accessed | tf_op | source)
XLA Modules:
  0.0 144.6 jit_solution(5565657320238000165)
XLA Ops:
  0.6 1.6 %slice.3.tail_ref = bf16[32,2048]{1,0:T(8,128)(2,1)} slice(bf16[1187,2048]{1,0:T(8,128)(2,1)} %table_hbm.1), slice={[1155:1187], [0:2048]} | slice | bytes 262144 | tf_op jit(solution)/shard_map/slice | solution.py:622
  2.2 139.6 %shard_map.77 = (bf16[64,512]{1,0:T(8,128)(2,1)}, f32[1,512]{1,0:T(1,128)}) custom-call(bf16[64,512]{1,0:T(8,128)(2,1)} %bitcast.5, f32[1,2048]{1,0:T(1,128)} %bitcast.7, f32[1,2048]{1,0:T(1,128)} %bitcast.8, bf16[2048,256]{1,0:T(8,128)(2,1)} %win_hbm.1, bf16[256,2048]{1,0:T(8,128)(2,1)} %wout_hbm.1, bf16[1187,2048]{1,0:T(8,128)(2,1)} %table_hbm.1, ...), custom_call_target="tpu_custom_call" | custom-call | tf_op jit(solution)/shard_map/pallas_call | solution.py:590
  141.9 1.5 %copy.10 = bf16[512,64]{0,1:T(8,128)(2,1)} copy(bf16[512,64]{0,1:T(8,128)(2,1)} %bitcast.6) | data formatting | bytes 131072
  143.4 1.2 copy.11

commit v3 on v2

--- a/solution.py
+++ b/solution.py
@@ -193,11 +193,12 @@
 GATHER, ADD = (True, True, False), (False, True, True)
 
 
-def feed_forward(links, me, other_core, x_ref, gin_ref, gout_ref, w_hbm, loads, refs, beside):
+def feed_forward(links, me, other_core, x_ref, gin_ref, gout_ref, w_hbm, loads, refs, beside, beside_done):
     xp, xs, win, wout, *refs = refs
     gathered, partial = refs[0:2], refs[2:4]
     n = (len(refs) - 4) // 2
     stages = [by_phase(FFN_ADD, refs[4 + n * k : 4 + n * k + n]) for k in range(2)]
+    done = beside_done
     y_lo, half = lax.rem(me["y"], 2), lax.div(me["y"], 2)
     opposite = moved(me, "y", 2)
     cross = moved(me, "y", 2 * y_lo - 1)
@@ -225,6 +226,11 @@
             passed[n].wait_recv()
             last.append(links.send(ref.at[1, next_to], ref.at[1, next_to], other_core))
 
+        def settle(what, *which):
+            for n in which:
+                last[n].wait_recv()
+            done.add(what)
+
         for n, (ref, _, own, _) in enumerate(jobs):
             yield
             got[n].wait_recv()
@@ -232,11 +238,12 @@
             last.append(links.send(ref.at[1, own], ref.at[1, own], other_core))
             if n >= 1:
                 hand_over(n - 1)
+            if n == 3:
+                settle("w_in", 0, 1, 2, 4)
         yield
         hand_over(len(jobs) - 1)
         yield
-        for copy in last:
-            copy.wait_recv()
+        settle("w_out", 3, 5, 6, 7)
 
     lanes = lax.broadcasted_iota(jnp.int32, (256, 128), 1) < 64
 
@@ -262,50 +269,55 @@
                     streams.remove(stream)
             if streams:
                 yield
-
-    run(
-        exchange_frames(),
-        exchange_weights(),
-        *beside,
-    )
-    few = lax.broadcasted_iota(jnp.int32, (128, 128), 1) < 64
-
-    def unpack(p, squares):
-        x, z = lax.div(p, 2), lax.rem(p, 2) * 2
-        at = pl.multiple_of(p * 128, 128)
-        sums = []
-        for k in range(2):
-            ref = gathered[k]
-            a, b = (ref[z, x], ref[z + 1, x]) if k == 0 else (ref[x, z], ref[x, z + 1])
-            a, b = a.astype(F32), b.astype(F32)
-            rows = slice(128 * k, 128 * k + 128)
-            top = jnp.where(few, a, pltpu.roll(b, 64, 1))
-            low = jnp.where(few, pltpu.roll(a, 64, 1), b)
-            xs[rows, pl.ds(at, 128)] = top.astype(BF16)
-            xs[rows, pl.ds(at + 1024, 128)] = low.astype(BF16)
-            sums.append(squares[k] + a * a + b * b)
-        return tuple(sums)
-
-    squares = lax.fori_loop(0, 8, unpack, (jnp.zeros((128, 128), F32),) * 2)
-    mean_sq = jnp.sum(jnp.concatenate(squares, axis=0), axis=1, keepdims=True) * (1.0 / D)
-    normed = (xs[...].astype(F32) * lax.rsqrt(mean_sq + 1e-06) * gin_ref[...]).astype(BF16)
-    for load in loads:
-        load.wait()
-    hidden = [
-        jax.nn.gelu(
-            jnp.dot(normed, win[w], preferred_element_type=F32), approximate=True
-        ).astype(BF16)
-        for w in range(2)
-    ]
-    for k, order in enumerate(FFN_ORDERS):
-        for part in range(2):
-            cols = slice(1024 * k + 512 * part, 1024 * k + 512 * part + 512)
-            block = jnp.dot(hidden[0], wout[0, :, cols], preferred_element_type=F32) + jnp.dot(
-                hidden[1], wout[1, :, cols], preferred_element_type=F32
-            )
-            for t in range(16):
-                at = (t // 4, t % 4) if order == "xz" else (t % 4, t // 4)
-                partial[k][(*at, ALL, slice(512 * part, 512 * part + 512))] = block[16 * t : 16 * t + 16]
+        done.add("frames")
+
+    def compute():
+        while "frames" not in done:
+            yield
+        few = lax.broadcasted_iota(jnp.int32, (128, 128), 1) < 64
+
+        def unpack(p, squares):
+            x, z = lax.div(p, 2), lax.rem(p, 2) * 2
+            at = pl.multiple_of(p * 128, 128)
+            sums = []
+            for k in range(2):
+                ref = gathered[k]
+                a, b = (ref[z, x], ref[z + 1, x]) if k == 0 else (ref[x, z], ref[x, z + 1])
+                a, b = a.astype(F32), b.astype(F32)
+                rows = slice(128 * k, 128 * k + 128)
+                top = jnp.where(few, a, pltpu.roll(b, 64, 1))
+                low = jnp.where(few, pltpu.roll(a, 64, 1), b)
+                xs[rows, pl.ds(at, 128)] = top.astype(BF16)
+                xs[rows, pl.ds(at + 1024, 128)] = low.astype(BF16)
+                sums.append(squares[k] + a * a + b * b)
+            return tuple(sums)
+
+        squares = lax.fori_loop(0, 8, unpack, (jnp.zeros((128, 128), F32),) * 2)
+        mean_sq = jnp.sum(jnp.concatenate(squares, axis=0), axis=1, keepdims=True) * (1.0 / D)
+        normed = (xs[...].astype(F32) * lax.rsqrt(mean_sq + 1e-06) * gin_ref[...]).astype(BF16)
+        while "w_in" not in done:
+            yield
+        for load in loads:
+            load.wait()
+        hidden = [
+            jax.nn.gelu(
+                jnp.dot(normed, win[w], preferred_element_type=F32), approximate=True
+            ).astype(BF16)
+            for w in range(2)
+        ]
+        while "w_out" not in done:
+            yield
+        for k, order in enumerate(FFN_ORDERS):
+            for part in range(2):
+                cols = slice(1024 * k + 512 * part, 1024 * k + 512 * part + 512)
+                block = jnp.dot(hidden[0], wout[0, :, cols], preferred_element_type=F32) + jnp.dot(
+                    hidden[1], wout[1, :, cols], preferred_element_type=F32
+                )
+                for t in range(16):
+                    at = (t // 4, t % 4) if order == "xz" else (t % 4, t // 4)
+                    partial[k][(*at, ALL, slice(512 * part, 512 * part + 512))] = block[16 * t : 16 * t + 16]
+
+    run(exchange_frames(), exchange_weights(), *beside, compute())
     found = {}
     run(
         *(
@@ -343,7 +355,7 @@
 
 def kernel(
     x_ref, gin_ref, gout_ref, win_hbm, wout_hbm, table_hbm, tail_ref, out_ref, log_ref,
-    turned, pieces, lat, scores, weights, stats, got_stats, factors, fin,
+    turned, pieces, lat, scores, weights, stats, got_stats, peaks, totals, fin,
     *rest,
 ):
     ffn_refs, rest = rest[: len(FFN_SCRATCH)], rest[len(FFN_SCRATCH) :]
@@ -368,7 +380,7 @@
     other_core = device({**me, "c": 1 - me["c"]})
     greet([moved(me, d, s) for d in ("x", "y", "z") for s in (1, -1, 2)] + [other_core])
     links = Links(ssem, rsem)
-    swaps = []
+    swaps, weights_done = [], set()
 
     def turn_table():
         yield
@@ -385,11 +397,13 @@
                 coming.append(load_piece(p + 2))
             if p < 4:
                 yield
+        while "w_out" not in weights_done:
+            yield
         swaps.append(links.send(turned.at[0], turned.at[1], other_core))
 
     latent = feed_forward(
         links, me, other_core, x_ref, gin_ref, gout_ref, (win_hbm, wout_hbm), (load_in, load_out),
-        ffn_refs, (turn_table(),),
+        ffn_refs, (turn_table(),), weights_done,
     )
     for s in range(2):
         for buf, order, (start, width) in zip(buffers[s], ORDERS, SPLITS):
@@ -407,7 +421,7 @@
             yield
         yield from stream
 
-    scale = 5.0 / math.sqrt(D)
+    scale = 5.0 / math.sqrt(D) * math.log2(math.e)
 
     def collect(s):
         def block(t, _):
@@ -420,39 +434,52 @@
 
         lax.fori_loop(0, 64, block, 0)
 
-    def score(s, g):
+    tile_lane = lax.broadcasted_iota(jnp.int32, (1, 256), 1)
+
+    def score_tile(s, g, t):
         frames = lat[:, g, :, :, :, 1024 * s : 1024 * s + 1024].reshape(512, 1024)
-
-        def tile(t, _):
-            half, n = lax.div(t, 5), lax.rem(t, 5)
-            cols = pl.ds(pl.multiple_of(n * 256, 256), 256)
-            at = pl.ds(pl.multiple_of(t * 256, 256), 256)
-            product = jnp.dot(
-                frames, turned[half, 1024 * s : 1024 * s + 1024, cols], preferred_element_type=F32
-            )
-            scores[g, :, at] = product if s == 0 else scores[g, :, at] + product
+        half, n = lax.div(t, 5), lax.rem(t, 5)
+        cols = pl.ds(pl.multiple_of(n * 256, 256), 256)
+        at = pl.ds(pl.multiple_of(t * 256, 256), 256)
+        product = jnp.dot(
+            frames, turned[half, 1024 * s : 1024 * s + 1024, cols], preferred_element_type=F32
+        )
+        if s == 0:
+            scores[g, :, at] = product
+            return
+        place = tile_lane + n * 256
+        real = (place < TAIL) | ((place >= TAIL + AGAIN) & (place < TAIL + REST))
+        value = jnp.where(real, (scores[g, :, at] + product) * scale, -1e30)
+        scores[g, :, at] = value
+        peaks[g] = jnp.maximum(peaks[g], jnp.maximum(value[:, :128], value[:, 128:]))
+
+    def find_peaks(g):
+        peaks[g] = jnp.broadcast_to(jnp.max(peaks[g], axis=1, keepdims=True), (512, 128))
+        totals[g] = jnp.zeros((512, 128), F32)
+
+    def weigh(g, rows, first, tiles):
+        top = peaks[g, rows]
+        total = totals[g, rows]
+        for c in range(tiles):
+            at = pl.ds(pl.multiple_of(first + 128 * c, 128), 128)
+            e = jnp.exp2(scores[g, rows, at] - top)
+            weights[g, rows, at] = e.astype(BF16)
+            total = total + e
+        totals[g, rows] = total
+
+    def local_stats(g):
+        stats[g, 0, 0:1] = peaks[g].T[0:1]
+        total = jnp.broadcast_to(jnp.sum(totals[g], axis=1, keepdims=True), (512, 128))
+        stats[g, 0, 1:2] = total.T[0:1]
+        done.add(f"local{g}")
+
+    def loop(first, last, *bodies):
+        def step(t, _):
+            for body in bodies:
+                body(t)
             return 0
 
-        lax.fori_loop(0, 10, tile, 0)
-
-    lane_id = lax.broadcasted_iota(jnp.int32, (1, 2 * WIDE), 1)
-    place = lax.rem(lane_id, WIDE)
-    real = (place < TAIL) | ((place >= TAIL + AGAIN) & (place < TAIL + REST))
-
-    def softmax(g):
-        def rows(r, _):
-            at = pl.ds(pl.multiple_of(r * 32, 32), 32)
-            s = jnp.where(real, scores[g, at, :] * scale, -1e30)
-            top = jnp.max(s, axis=1, keepdims=True)
-            e = jnp.exp(s - top)
-            weights[g, at, :] = e.astype(BF16)
-            factors[0, at, :] = jnp.broadcast_to(top, (32, 128))
-            factors[1, at, :] = jnp.broadcast_to(jnp.sum(e, axis=1, keepdims=True), (32, 128))
-            return 0
-
-        lax.fori_loop(0, 16, rows, 0)
-        stats[g, 0, 0:1] = factors[0].T[0:1]
-        stats[g, 0, 1:2] = factors[1].T[0:1]
+        lax.fori_loop(first, last, step, 0)
 
     def share_stats(g):
         for phase, dim in enumerate("xyz"):
@@ -466,26 +493,21 @@
             pairs = [stats[g, phase]] + [got_stats[g, 3 * phase + n] for n in range(3)]
             top = functools.reduce(jnp.maximum, [p[0:1] for p in pairs])
             stats[g, phase + 1, 0:1] = top
-            stats[g, phase + 1, 1:2] = sum(p[1:2] * jnp.exp(p[0:1] - top) for p in pairs)
-
-    def mix(g, n):
-        rows = slice(512 * n, 512 * n + 512)
+            stats[g, phase + 1, 1:2] = sum(p[1:2] * jnp.exp2(p[0:1] - top) for p in pairs)
+
+    def mix_tile(g, t):
+        n, q = lax.div(t, 2), lax.rem(t, 2)
+        rows = pl.ds(pl.multiple_of(n * 512, 512), 512)
+        frames = pl.ds(pl.multiple_of(q * 256, 256), 256)
         dims = (((1,), (1,)), ((), ()))
-
-        def tile(q, _):
-            frames = pl.ds(pl.multiple_of(q * 256, 256), 256)
-            total = lax.dot_general(
-                turned[0, rows, :], weights[g, frames, 0:WIDE], dims, preferred_element_type=F32
-            ) + lax.dot_general(
-                turned[1, rows, :], weights[g, frames, WIDE:], dims, preferred_element_type=F32
-            )
-            scores[g, :, pl.ds(pl.multiple_of(512 * n + q * 256, 256), 256)] = total
-            return 0
-
-        lax.fori_loop(0, 2, tile, 0)
+        scores[g, :, pl.ds(pl.multiple_of(t * 256, 256), 256)] = lax.dot_general(
+            turned[0, rows, :], weights[g, frames, 0:WIDE], dims, preferred_element_type=F32
+        ) + lax.dot_general(
+            turned[1, rows, :], weights[g, frames, WIDE:], dims, preferred_element_type=F32
+        )
 
     def rescale(g):
-        factor = jnp.exp(stats[g, 0, 0:1] - stats[g, 3, 0:1])
+        factor = jnp.exp2(stats[g, 0, 0:1] - stats[g, 3, 0:1])
 
         def block(h8, _):
             for n in range(4):
@@ -515,26 +537,35 @@
         swaps[0].wait_recv()
         collect(0)
         for g in range(2):
-            score(0, g)
+            loop(0, 10, functools.partial(score_tile, 0, g))
+            peaks[g] = jnp.full((512, 128), -1e30, F32)
             yield
         yield from wait_for(*(f"lat1{k}" for k in range(3)))
         collect(1)
         links.drain()
-        for g in range(2):
-            score(1, g)
-            softmax(g)
-            done.add(f"local{g}")
-            yield
-        for n in range(4):
-            mix(0, n)
-            if n % 2:
-                yield
+        loop(0, 10, functools.partial(score_tile, 1, 0))
+        find_peaks(0)
+        loop(
+            0, 10, functools.partial(score_tile, 1, 1), lambda t: weigh(0, ALL, t * 256, 2)
+        )
+        local_stats(0)
+        yield
+        find_peaks(1)
+        for part in range(2):
+            loop(
+                4 * part, 4 * part + 4, functools.partial(mix_tile, 0),
+                lambda t: weigh(1, pl.ds(pl.multiple_of(t * 64, 64), 64), 0, 20),
+            )
+            if part == 1:
+                local_stats(1)
+            yield
         yield from wait_for("stats0")
         rescale(0)
         done.add("sums0")
         yield
-        for n in range(4):
-            mix(1, n)
+        for part in range(2):
+            loop(4 * part, 4 * part + 4, functools.partial(mix_tile, 1))
+            yield
         yield from wait_for("stats1")
         rescale(1)
         done.add("sums1")
@@ -548,7 +579,7 @@
                 out_ref[16 * j : 16 * j + 16, 256 * g : 256 * g + 256] = (
                     fin[g, :, 256 * j : 256 * j + 256] / total
                 ).astype(BF16)
-            log_ref[:, 256 * g : 256 * g + 256] = top + jnp.log(total)
+            log_ref[:, 256 * g : 256 * g + 256] = top * math.log(2.0) + jnp.log(total)
 
     def delayed(stream, rounds):
         for _ in range(rounds):
@@ -604,6 +635,7 @@
             pltpu.VMEM((2, 4, 8, 512), F32),
             pltpu.VMEM((2, 9, 8, 512), F32),
             pltpu.VMEM((2, 512, 128), F32),
+            pltpu.VMEM((2, 512, 128), F32),
             pltpu.VMEM((2, 16, 1024), F32),
             *FFN_SCRATCH,
             *buffers,

time: 145 us -> 147 us (1.014)
  Pallas kernels: 140 us -> 142 us
    pallas_call x1, Pallas kernels: 140 us -> 142 us  [fused(): pl.pallas_call(kernel, out_shape=(jax.ShapeDtypeStruct((64, 512), BF16),...]
where the time goes in v3:
time: 147 us
  Pallas kernels  142 us (97%)
  local copies, waits for them, and re-layouts  4.31 us (3%)
    pallas_call x1, Pallas kernels, fused(): pl.pallas_call(kernel, out_shape=(jax.ShapeDtypeStruct((64, 512), BF16),...  142 us

profile of v3, /device:TPU:0, one launch (start us, length us, event | category | flops | bytes accessed | tf_op | source)
XLA Modules:
  0.0 146.9 jit_solution(16182804083509319202)
XLA Ops:
  0.6 1.6 %slice.3.tail_ref = bf16[32,2048]{1,0:T(8,128)(2,1)} slice(bf16[1187,2048]{1,0:T(8,128)(2,1)} %table_hbm.1), slice={[1155:1187], [0:2048]} | slice | bytes 262144 | tf_op jit(solution)/shard_map/slice | solution.py:654
  2.2 142.0 %shard_map.77 = (bf16[64,512]{1,0:T(8,128)(2,1)}, f32[1,512]{1,0:T(1,128)}) custom-call(bf16[64,512]{1,0:T(8,128)(2,1)} %bitcast.5, f32[1,2048]{1,0:T(1,128)} %bitcast.7, f32[1,2048]{1,0:T(1,128)} %bitcast.8, bf16[2048,256]{1,0:T(8,128)(2,1)} %win_hbm.1, bf16[256,2048]{1,0:T(8,128)(2,1)} %wout_hbm.1, bf16[1187,2048]{1,0:T(8,128)(2,1)} %table_hbm.1, ...), custom_call_target="tpu_custom_call" | custom-call | tf_op jit(solution)/shard_map/pallas_call | solution.py:621
  144.2 1.5 %copy.10 = bf16[512,64]{0,1:T(8,128)(2,1)} copy(bf16[512,64]{0,1:T(8,128)(2,1)} %bitcast.6) | data formatting | bytes 131072
  145.7 1.2 copy.11

commit v4 on v3

--- a/solution.py
+++ b/solution.py
@@ -15,6 +15,7 @@
 REST = 32
 AGAIN = REST - (ROWS - TAIL)
 WIDE = 1280
+SCORE = 1280
 F32 = jnp.float32
 BF16 = jnp.bfloat16
 ALL = slice(None)
@@ -355,7 +356,7 @@
 
 def kernel(
     x_ref, gin_ref, gout_ref, win_hbm, wout_hbm, table_hbm, tail_ref, out_ref, log_ref,
-    turned, pieces, lat, scores, weights, stats, got_stats, peaks, totals, fin,
+    turned, pieces, lat, scores, weights, stats, got_stats, sums, peaks, totals, fin,
     *rest,
 ):
     ffn_refs, rest = rest[: len(FFN_SCRATCH)], rest[len(FFN_SCRATCH) :]
@@ -423,35 +424,33 @@
 
     scale = 5.0 / math.sqrt(D) * math.log2(math.e)
 
-    def collect(s):
+    def collect():
         def block(t, _):
             at = {"y": lax.div(t, 16), "x": lax.rem(lax.div(t, 4), 4), "z": lax.rem(t, 4)}
             to = (lax.rem(at["y"], 2), lax.div(at["y"], 2), at["x"], at["z"])
-            for buf, order, (start, width) in zip(buffers[s], ORDERS, SPLITS):
-                cols = slice(1024 * s + start, 1024 * s + start + width)
-                lat[(*to, ALL, cols)] = buf[tuple(at[d] for d in reversed(order))]
+            for s in range(2):
+                for buf, order, (start, width) in zip(buffers[s], ORDERS, SPLITS):
+                    cols = slice(1024 * s + start, 1024 * s + start + width)
+                    lat[(*to, ALL, cols)] = buf[tuple(at[d] for d in reversed(order))]
             return 0
 
         lax.fori_loop(0, 64, block, 0)
 
-    tile_lane = lax.broadcasted_iota(jnp.int32, (1, 256), 1)
-
-    def score_tile(s, g, t):
-        frames = lat[:, g, :, :, :, 1024 * s : 1024 * s + 1024].reshape(512, 1024)
-        half, n = lax.div(t, 5), lax.rem(t, 5)
-        cols = pl.ds(pl.multiple_of(n * 256, 256), 256)
-        at = pl.ds(pl.multiple_of(t * 256, 256), 256)
-        product = jnp.dot(
-            frames, turned[half, 1024 * s : 1024 * s + 1024, cols], preferred_element_type=F32
+    tile_lane = lax.broadcasted_iota(jnp.int32, (1, SCORE), 1)
+
+    def score_tile(g, t):
+        frames = lat[:, g].reshape(512, D)
+        half, n = lax.div(t, WIDE // SCORE), lax.rem(t, WIDE // SCORE)
+        cols = pl.ds(pl.multiple_of(n * SCORE, 128), SCORE)
+        at = pl.ds(pl.multiple_of(t * SCORE, 128), SCORE)
+        place = tile_lane + n * SCORE
+        real = (place < TAIL) | ((place >= TAIL + AGAIN) & (place < TAIL + REST))
+        product = jnp.dot(frames, turned[half, :, cols], preferred_element_type=F32)
+        value = jnp.where(real, product * scale, -1e30)
+        scores[g, :, at] = value
+        peaks[g] = functools.reduce(
+            jnp.maximum, [peaks[g]] + [value[:, c : c + 128] for c in range(0, SCORE, 128)]
         )
-        if s == 0:
-            scores[g, :, at] = product
-            return
-        place = tile_lane + n * 256
-        real = (place < TAIL) | ((place >= TAIL + AGAIN) & (place < TAIL + REST))
-        value = jnp.where(real, (scores[g, :, at] + product) * scale, -1e30)
-        scores[g, :, at] = value
-        peaks[g] = jnp.maximum(peaks[g], jnp.maximum(value[:, :128], value[:, 128:]))
 
     def find_peaks(g):
         peaks[g] = jnp.broadcast_to(jnp.max(peaks[g], axis=1, keepdims=True), (512, 128))
@@ -467,11 +466,13 @@
             total = total + e
         totals[g, rows] = total
 
-    def local_stats(g):
-        stats[g, 0, 0:1] = peaks[g].T[0:1]
+    def local_top(g):
+        stats[0, g, 0, 0:1] = peaks[g].T[0:1]
+        done.add(f"peak{g}")
+
+    def local_sum(g):
         total = jnp.broadcast_to(jnp.sum(totals[g], axis=1, keepdims=True), (512, 128))
-        stats[g, 0, 1:2] = total.T[0:1]
-        done.add(f"local{g}")
+        sums[g] = total.T[0:1]
 
     def loop(first, last, *bodies):
         def step(t, _):
@@ -481,33 +482,35 @@
 
         lax.fori_loop(first, last, step, 0)
 
-    def share_stats(g):
+    def share(g, kind, combine):
         for phase, dim in enumerate("xyz"):
             copies = [
-                links.send(stats.at[g, phase], got_stats.at[g, 3 * phase + n], moved(me, dim, s))
+                links.send(
+                    stats.at[kind, g, phase], got_stats.at[kind, g, 3 * phase + n], moved(me, dim, s)
+                )
                 for n, s in enumerate((1, -1, 2))
             ]
             yield
             for copy in copies:
                 copy.wait_recv()
-            pairs = [stats[g, phase]] + [got_stats[g, 3 * phase + n] for n in range(3)]
-            top = functools.reduce(jnp.maximum, [p[0:1] for p in pairs])
-            stats[g, phase + 1, 0:1] = top
-            stats[g, phase + 1, 1:2] = sum(p[1:2] * jnp.exp2(p[0:1] - top) for p in pairs)
+            parts = [stats[kind, g, phase]] + [got_stats[kind, g, 3 * phase + n] for n in range(3)]
+            stats[kind, g, phase + 1] = functools.reduce(combine, parts)
+
+    def share_sum(g):
+        stats[1, g, 0, 0:1] = sums[g] * jnp.exp2(stats[0, g, 0, 0:1] - stats[0, g, 3, 0:1])
+        yield from share(g, 1, jnp.add)
 
     def mix_tile(g, t):
-        n, q = lax.div(t, 2), lax.rem(t, 2)
-        rows = pl.ds(pl.multiple_of(n * 512, 512), 512)
-        frames = pl.ds(pl.multiple_of(q * 256, 256), 256)
+        rows = pl.ds(pl.multiple_of(t * 512, 512), 512)
         dims = (((1,), (1,)), ((), ()))
-        scores[g, :, pl.ds(pl.multiple_of(t * 256, 256), 256)] = lax.dot_general(
-            turned[0, rows, :], weights[g, frames, 0:WIDE], dims, preferred_element_type=F32
+        scores[g, :, pl.ds(pl.multiple_of(t * 512, 512), 512)] = lax.dot_general(
+            turned[0, rows, :], weights[g, :, 0:WIDE], dims, preferred_element_type=F32
         ) + lax.dot_general(
-            turned[1, rows, :], weights[g, frames, WIDE:], dims, preferred_element_type=F32
+            turned[1, rows, :], weights[g, :, WIDE:], dims, preferred_element_type=F32
         )
 
     def rescale(g):
-        factor = jnp.exp2(stats[g, 0, 0:1] - stats[g, 3, 0:1])
+        factor = jnp.exp2(stats[0, g, 0, 0:1] - stats[0, g, 3, 0:1])
 
         def block(h8, _):
             for n in range(4):
@@ -533,38 +536,38 @@
             yield
 
     def compute():
-        yield from wait_for(*(f"lat0{k}" for k in range(3)))
+        yield from wait_for(*(f"lat{s}{k}" for s in range(2) for k in range(3)))
         swaps[0].wait_recv()
-        collect(0)
-        for g in range(2):
-            loop(0, 10, functools.partial(score_tile, 0, g))
-            peaks[g] = jnp.full((512, 128), -1e30, F32)
-            yield
-        yield from wait_for(*(f"lat1{k}" for k in range(3)))
-        collect(1)
+        collect()
         links.drain()
-        loop(0, 10, functools.partial(score_tile, 1, 0))
+        peaks[...] = jnp.full((2, 512, 128), -1e30, F32)
+        tiles = 2 * WIDE // SCORE
+        loop(0, tiles, functools.partial(score_tile, 0))
         find_peaks(0)
+        local_top(0)
+        yield
         loop(
-            0, 10, functools.partial(score_tile, 1, 1), lambda t: weigh(0, ALL, t * 256, 2)
+            0, tiles, functools.partial(score_tile, 1),
+            lambda t: weigh(0, ALL, t * SCORE, SCORE // 128),
         )
-        local_stats(0)
-        yield
+        local_sum(0)
         find_peaks(1)
+        local_top(1)
+        yield
         for part in range(2):
             loop(
-                4 * part, 4 * part + 4, functools.partial(mix_tile, 0),
-                lambda t: weigh(1, pl.ds(pl.multiple_of(t * 64, 64), 64), 0, 20),
+                2 * part, 2 * part + 2, functools.partial(mix_tile, 0),
+                lambda t: weigh(1, pl.ds(pl.multiple_of(t * 128, 128), 128), 0, 20),
             )
             if part == 1:
-                local_stats(1)
+                local_sum(1)
             yield
         yield from wait_for("stats0")
         rescale(0)
         done.add("sums0")
         yield
         for part in range(2):
-            loop(4 * part, 4 * part + 4, functools.partial(mix_tile, 1))
+            loop(2 * part, 2 * part + 2, functools.partial(mix_tile, 1))
             yield
         yield from wait_for("stats1")
         rescale(1)
@@ -572,27 +575,24 @@
 
     def final():
         for g in range(2):
-            yield from wait_for(*(f"out{g}{k}" for k in range(3)))
+            yield from wait_for(f"total{g}", *(f"out{g}{k}" for k in range(3)))
             lanes = pl.ds(pl.multiple_of(y_lo * 256, 256), 256)
-            top, total = stats[g, 3, 0:1, lanes], stats[g, 3, 1:2, lanes]
+            top, total = stats[0, g, 3, 0:1, lanes], stats[1, g, 3, 0:1, lanes]
             for j in range(4):
                 out_ref[16 * j : 16 * j + 16, 256 * g : 256 * g + 256] = (
                     fin[g, :, 256 * j : 256 * j + 256] / total
                 ).astype(BF16)
             log_ref[:, 256 * g : 256 * g + 256] = top * math.log(2.0) + jnp.log(total)
 
-    def delayed(stream, rounds):
-        for _ in range(rounds):
-            yield
-        yield from stream
-
     streams = [
-        then(delayed(gather_stream(links, me, buffers[s][k], o, GATHER), 2 * s), f"lat{s}{k}")
+        then(gather_stream(links, me, buffers[s][k], o, GATHER), f"lat{s}{k}")
         for s in range(2)
         for k, o in enumerate(ORDERS)
     ]
     streams.append(compute())
-    streams += [then(after([f"local{g}"], share_stats(g)), f"stats{g}") for g in range(2)]
+    for g in range(2):
+        streams.append(then(after([f"peak{g}"], share(g, 0, jnp.maximum)), f"stats{g}"))
+        streams.append(then(after([f"sums{g}"], share_sum(g)), f"total{g}"))
     for g in range(2):
         for k, (o, (start, width)) in enumerate(zip(ORDERS, SPLITS)):
             def result(value, g=g, start=start, width=width):
@@ -612,7 +612,7 @@
 def fused(frames_in, in_gain, out_gain, w_in, w_out, table, tail):
     vmem = pl.BlockSpec(memory_space=pltpu.VMEM)
     hbm = pl.BlockSpec(memory_space=pl.ANY)
-    copies = FFN_COPIES + 1 + 2 * 9 + 2 * 3 * 2 * 12
+    copies = FFN_COPIES + 1 + 2 * 18 + 2 * 3 * 2 * 12
     buffers, stages = [], []
     for _ in range(2):
         for _, width in SPLITS:
@@ -632,8 +632,9 @@
             pltpu.VMEM((2, 2, 4, 4, 16, D), BF16),
             pltpu.VMEM((2, 512, 2 * WIDE), F32),
             pltpu.VMEM((2, 512, 2 * WIDE), BF16),
-            pltpu.VMEM((2, 4, 8, 512), F32),
-            pltpu.VMEM((2, 9, 8, 512), F32),
+            pltpu.VMEM((2, 2, 4, 1, 512), F32),
+            pltpu.VMEM((2, 2, 9, 1, 512), F32),
+            pltpu.VMEM((2, 1, 512), F32),
             pltpu.VMEM((2, 512, 128), F32),
             pltpu.VMEM((2, 512, 128), F32),
             pltpu.VMEM((2, 16, 1024), F32),

time: 147 us -> 137 us (0.932)
  Pallas kernels: 142 us -> 132 us
    pallas_call x1, Pallas kernels: 142 us -> 132 us  [fused(): pl.pallas_call(kernel, out_shape=(jax.ShapeDtypeStruct((64, 512), BF16),...]
where the time goes in v4:
time: 137 us; the launch traced here: 136 us
  Pallas kernels  132 us (96%)
  local copies, waits for them, and re-layouts  4.31 us (3%)
    pallas_call x1, Pallas kernels, fused(): pl.pallas_call(kernel, out_shape=(jax.ShapeDtypeStruct((64, 512), BF16),...  132 us

profile of v4, /device:TPU:0, one launch (start us, length us, event | category | flops | bytes accessed | tf_op | source)
XLA Modules:
  0.0 136.5 jit_solution(13690183407842536626)
XLA Ops:
  0.6 1.6 %slice.3.tail_ref = bf16[32,2048]{1,0:T(8,128)(2,1)} slice(bf16[1187,2048]{1,0:T(8,128)(2,1)} %table_hbm.1), slice={[1155:1187], [0:2048]} | slice | bytes 262144 | tf_op jit(solution)/shard_map/slice | solution.py:655
  2.2 131.5 %shard_map.77 = (bf16[64,512]{1,0:T(8,128)(2,1)}, f32[1,512]{1,0:T(1,128)}) custom-call(bf16[64,512]{1,0:T(8,128)(2,1)} %bitcast.5, f32[1,2048]{1,0:T(1,128)} %bitcast.7, f32[1,2048]{1,0:T(1,128)} %bitcast.8, bf16[2048,256]{1,0:T(8,128)(2,1)} %win_hbm.1, bf16[256,2048]{1,0:T(8,128)(2,1)} %wout_hbm.1, bf16[1187,2048]{1,0:T(8,128)(2,1)} %table_hbm.1, ...), custom_call_target="tpu_custom_call" | custom-call | tf_op jit(solution)/shard_map/pallas_call | solution.py:621
  133.8 1.5 %copy.10 = bf16[512,64]{0,1:T(8,128)(2,1)} copy(bf16[512,64]{0,1:T(8,128)(2,1)} %bitcast.6) | data formatting | bytes 131072
  135.2 1.2 copy.11

commit v5 on v4

--- a/solution.py
+++ b/solution.py
@@ -501,13 +501,16 @@
         yield from share(g, 1, jnp.add)
 
     def mix_tile(g, t):
-        rows = pl.ds(pl.multiple_of(t * 512, 512), 512)
+        rows = pl.ds(pl.multiple_of(t * 1024, 1024), 1024)
         dims = (((1,), (1,)), ((), ()))
-        scores[g, :, pl.ds(pl.multiple_of(t * 512, 512), 512)] = lax.dot_general(
+        total = lax.dot_general(
             turned[0, rows, :], weights[g, :, 0:WIDE], dims, preferred_element_type=F32
         ) + lax.dot_general(
             turned[1, rows, :], weights[g, :, WIDE:], dims, preferred_element_type=F32
         )
+        for n in range(2):
+            lanes = pl.ds(pl.multiple_of(t * 1024 + 512 * n, 512), 512)
+            scores[g, :, lanes] = total[512 * n : 512 * n + 512]
 
     def rescale(g):
         factor = jnp.exp2(stats[0, g, 0, 0:1] - stats[0, g, 3, 0:1])
@@ -556,8 +559,8 @@
         yield
         for part in range(2):
             loop(
-                2 * part, 2 * part + 2, functools.partial(mix_tile, 0),
-                lambda t: weigh(1, pl.ds(pl.multiple_of(t * 128, 128), 128), 0, 20),
+                part, part + 1, functools.partial(mix_tile, 0),
+                lambda t: weigh(1, pl.ds(pl.multiple_of(t * 256, 256), 256), 0, 20),
             )
             if part == 1:
                 local_sum(1)
@@ -567,8 +570,7 @@
         done.add("sums0")
         yield
         for part in range(2):
-            loop(2 * part, 2 * part + 2, functools.partial(mix_tile, 1))
-            yield
+            loop(part, part + 1, functools.partial(mix_tile, 1))
         yield from wait_for("stats1")
         rescale(1)
         done.add("sums1")

time: 137 us -> 130 us (0.949)
  Pallas kernels: 132 us -> 125 us
    pallas_call x1, Pallas kernels: 132 us -> 125 us  [fused(): pl.pallas_call(kernel, out_shape=(jax.ShapeDtypeStruct((64, 512), BF16),...]
where the time goes in v5:
time: 130 us
  Pallas kernels  125 us (96%)
  local copies, waits for them, and re-layouts  4.31 us (3%)
    pallas_call x1, Pallas kernels, fused(): pl.pallas_call(kernel, out_shape=(jax.ShapeDtypeStruct((64, 512), BF16),...  125 us
    unnamed x2, local copies, waits for them, and re-layouts  2.71 us

profile of v5, /device:TPU:0, one launch (start us, length us, event | category | flops | bytes accessed | tf_op | source)
XLA Modules:
  0.0 130.3 jit_solution(11870846887417090081)
XLA Ops:
  0.6 1.6 %slice.3.tail_ref = bf16[32,2048]{1,0:T(8,128)(2,1)} slice(bf16[1187,2048]{1,0:T(8,128)(2,1)} %table_hbm.1), slice={[1155:1187], [0:2048]} | slice | bytes 262144 | tf_op jit(solution)/shard_map/slice | solution.py:657
  2.2 125.3 %shard_map.77 = (bf16[64,512]{1,0:T(8,128)(2,1)}, f32[1,512]{1,0:T(1,128)}) custom-call(bf16[64,512]{1,0:T(8,128)(2,1)} %bitcast.5, f32[1,2048]{1,0:T(1,128)} %bitcast.7, f32[1,2048]{1,0:T(1,128)} %bitcast.8, bf16[2048,256]{1,0:T(8,128)(2,1)} %win_hbm.1, bf16[256,2048]{1,0:T(8,128)(2,1)} %wout_hbm.1, bf16[1187,2048]{1,0:T(8,128)(2,1)} %table_hbm.1, ...), custom_call_target="tpu_custom_call" | custom-call | tf_op jit(solution)/shard_map/pallas_call | solution.py:623
  127.6 1.5 %copy.10 = bf16[512,64]{0,1:T(8,128)(2,1)} copy(bf16[512,64]{0,1:T(8,128)(2,1)} %bitcast.6) | data formatting | bytes 131072
  129.0 1.2 copy.11

commit v6 on v5

--- a/solution.py
+++ b/solution.py
@@ -542,7 +542,6 @@
         yield from wait_for(*(f"lat{s}{k}" for s in range(2) for k in range(3)))
         swaps[0].wait_recv()
         collect()
-        links.drain()
         peaks[...] = jnp.full((2, 512, 128), -1e30, F32)
         tiles = 2 * WIDE // SCORE
         loop(0, tiles, functools.partial(score_tile, 0))
@@ -566,6 +565,7 @@
                 local_sum(1)
             yield
         yield from wait_for("stats0")
+        links.drain()
         rescale(0)
         done.add("sums0")
         yield

time: 130 us -> 130 us (level)
  no operation moved by 1% of the time
where the time goes in v6:
time: 130 us
  Pallas kernels  125 us (96%)
  local copies, waits for them, and re-layouts  4.31 us (3%)
    pallas_call x1, Pallas kernels, fused(): pl.pallas_call(kernel, out_shape=(jax.ShapeDtypeStruct((64, 512), BF16),...  125 us
    unnamed x2, local copies, waits for them, and re-layouts  2.71 us

profile of v6, /device:TPU:0, one launch (start us, length us, event | category | flops | bytes accessed | tf_op | source)
XLA Modules:
  0.0 130.1 jit_solution(5321661806545063091)
XLA Ops:
  0.6 1.6 %slice.3.tail_ref = bf16[32,2048]{1,0:T(8,128)(2,1)} slice(bf16[1187,2048]{1,0:T(8,128)(2,1)} %table_hbm.1), slice={[1155:1187], [0:2048]} | slice | bytes 262144 | tf_op jit(solution)/shard_map/slice | solution.py:657
  2.2 125.2 %shard_map.77 = (bf16[64,512]{1,0:T(8,128)(2,1)}, f32[1,512]{1,0:T(1,128)}) custom-call(bf16[64,512]{1,0:T(8,128)(2,1)} %bitcast.5, f32[1,2048]{1,0:T(1,128)} %bitcast.7, f32[1,2048]{1,0:T(1,128)} %bitcast.8, bf16[2048,256]{1,0:T(8,128)(2,1)} %win_hbm.1, bf16[256,2048]{1,0:T(8,128)(2,1)} %wout_hbm.1, bf16[1187,2048]{1,0:T(8,128)(2,1)} %table_hbm.1, ...), custom_call_target="tpu_custom_call" | custom-call | tf_op jit(solution)/shard_map/pallas_call | solution.py:623
  127.4 1.5 %copy.10 = bf16[512,64]{0,1:T(8,128)(2,1)} copy(bf16[512,64]{0,1:T(8,128)(2,1)} %bitcast.6) | data formatting | bytes 131072
  128.9 1.2 copy.11
